TPU v7x, 256 devices: a whole 4x4x8 slice. The times are simulated.
256 devices in a mesh: shot: 16 (over z_lo, y, core), sub: 16 (over x, z_hi).
Axes of the slice: x: 4, y: 4, z: 8 (z_hi: 4, z_lo: 2; z = z_hi * 2 + z_lo), core: 2. Of those that a mesh axis runs over, the one named last changes fastest.
Arguments:
- velocity: float32 [512, 8, 64, 128], P(('shot', 'sub')), may hold values from 0.25 to 0.5
- tile_slot: int32 [512], replicated, may hold values from 0 to 511, each once
- anchors: int32 [16, 2], replicated, may hold values from 0 to 16, as said below
- source_cell: int32 [16], P('shot'), may hold values from 0 to 1048575
- wavelet: float32 [16, 8], P('shot'), may hold values from -24 to 24
- receiver_cells: int32 [16, 256], P('shot'), may hold values from 0 to 1048575
- observed: float32 [16, 8, 256], P('shot'), may hold values from -6 to 6
- fwd_prev: float32 [16, 128, 64, 128], P('shot', 'sub'), may hold values from -6 to 6
- fwd_curr: float32 [16, 128, 64, 128], P('shot', 'sub'), may hold values from -6 to 6
- adj_prev: float32 [16, 128, 64, 128], P('shot', 'sub'), may hold values from -6 to 6
- adj_curr: float32 [16, 128, 64, 128], P('shot', 'sub'), may hold values from -6 to 6
Outputs:
- gradient: float32 [512, 8, 64, 128], P(('shot', 'sub'))
Inputs may be any that keep to these rules, and one draw needn't show every extreme that they name: `anchors`: row g is shot g's aperture anchor: a tile index along the first dimension from 0 to 16, then one along the second from 0 to 15.
All inputs are finite; a program needn't handle non-finite values.
Results may differ from a plain program's by a relative error of at most 0.0003.
Values sent between devices are 32-bit elements; how exact they have to be, the bound alone decides.
No kernel may reach another device: no remote copies, remote signals or barrier semaphores. Data moves between devices by JAX's collectives and lax.ppermute only.
A program may use at most 64 MiB of HBM per device.

v0:
```python
import jax
import jax.numpy as jnp
from jax import lax
from jax.sharding import PartitionSpec as P


def padded_2(block, sides, width):
    for axis, dim in sides:
        count = lax.axis_size(axis)
        forward = [(i, i + 1) for i in range(count - 1)]
        backward = [(target, source) for source, target in forward]
        low = lax.ppermute(
            lax.slice_in_dim(block, block.shape[dim] - width, None, axis=dim), axis, forward
        )
        high = lax.ppermute(lax.slice_in_dim(block, 0, width, axis=dim), axis, backward)
        block = jnp.concatenate([low, block, high], axis=dim)
    return block


def slot_lookup(tile_slot, tile_ids):
    table = jnp.arange(tile_slot.shape[0], dtype=jnp.int32)
    return jnp.sum(jnp.where(table[None, :] == tile_ids[:, None], tile_slot[None, :], 0), axis=1)


def laplace(wavefield):
    halo_field = padded_2(wavefield, (("sub", 0),), 1)
    padded = jnp.pad(halo_field, ((0, 0), (1, 1), (1, 1)))
    summed = padded[2:, 1:-1, 1:-1] + padded[:-2, 1:-1, 1:-1]
    summed = summed + padded[1:-1, 2:, 1:-1] + padded[1:-1, :-2, 1:-1]
    summed = summed + padded[1:-1, 1:-1, 2:] + padded[1:-1, 1:-1, :-2]
    return summed - 6.0 * wavefield


def shards(
    velocity,
    tile_slot,
    anchors,
    source_cell,
    wavelet,
    receiver_cells,
    observed,
    fwd_prev,
    fwd_curr,
    adj_prev,
    adj_curr,
):
    n_shot = lax.axis_size("shot")
    n_sub = lax.axis_size("sub")
    group_index = lax.axis_index("shot")
    sub_index = lax.axis_index("sub")
    local_slots = velocity.shape[0]
    tile_shape = velocity.shape[1:]
    cell_count = tile_shape[0] * tile_shape[1] * tile_shape[2]
    flat_vel = velocity.reshape(local_slots, cell_count)
    own_anchor = lax.dynamic_slice_in_dim(anchors, group_index, 1, 0)[0]
    highest = lax.Precision.HIGHEST
    gathered = lax.all_gather(flat_vel, "shot", axis=0, tiled=True)
    row_ids = jnp.arange(local_slots * n_shot, dtype=jnp.int32)
    row_slot = (row_ids // local_slots * n_sub + sub_index) * local_slots + row_ids % local_slots
    wanted = slot_lookup(
        tile_slot, (own_anchor[0] + jnp.arange(n_sub, dtype=jnp.int32)) * n_shot + own_anchor[1]
    )
    selector = (wanted[:, None] == row_slot[None, :]).astype(jnp.float32)
    routed = jnp.dot(selector, gathered, precision=highest, preferred_element_type=jnp.float32)
    own_tile = lax.psum_scatter(routed, "sub", scatter_dimension=0, tiled=True)
    speed = own_tile.reshape(tile_shape)
    speed_sq = speed * speed
    src_offset = source_cell[0] - sub_index * cell_count
    src_valid = (src_offset >= 0) & (src_offset < cell_count)
    src_index = jnp.clip(src_offset, 0, cell_count - 1)
    rec_offset = receiver_cells[0] - sub_index * cell_count
    rec_valid = (rec_offset >= 0) & (rec_offset < cell_count)
    rec_index = jnp.clip(rec_offset, 0, cell_count - 1)
    step_count = wavelet.shape[1]
    previous, current = (fwd_prev[0], fwd_curr[0])
    laplacians = []
    residuals = []
    for time_step in range(step_count):
        laplacian = laplace(current)
        advanced = 2.0 * current - previous + speed_sq * laplacian
        amount = jnp.where(src_valid, wavelet[0, time_step], 0.0)
        advanced = advanced.reshape(-1).at[src_index].add(amount).reshape(tile_shape)
        sample = advanced.reshape(-1)[rec_index]
        residuals.append(jnp.where(rec_valid, sample - observed[0, time_step], 0.0))
        laplacians.append(laplacian)
        previous, current = (current, advanced)
    previous, current = (adj_prev[0], adj_curr[0])
    image_sum = jnp.zeros(tile_shape, jnp.float32)
    for back_step in range(step_count):
        advanced = 2.0 * current - previous + speed_sq * laplace(current)
        advanced = (
            advanced.reshape(-1)
            .at[rec_index]
            .add(residuals[step_count - 1 - back_step])
            .reshape(tile_shape)
        )
        image_sum = image_sum + speed * advanced * laplacians[step_count - 1 - back_step]
        previous, current = (current, advanced)
    shot_gradient = (2.0 / step_count * image_sum).reshape(1, cell_count)
    group_grads = lax.all_gather(shot_gradient, "sub", axis=0, tiled=True)
    own_wanted = slot_lookup(
        tile_slot, (own_anchor[0] + jnp.arange(n_sub, dtype=jnp.int32)) * n_shot + own_anchor[1]
    )
    slot_rows = jnp.arange(local_slots * lax.axis_size("shot"), dtype=jnp.int32)
    slot_ids = (
        slot_rows // local_slots * n_sub + sub_index
    ) * local_slots + slot_rows % local_slots
    picker = (slot_ids[:, None] == own_wanted[None, :]).astype(jnp.float32)
    summed_tiles = lax.psum_scatter(
        jnp.dot(picker, group_grads, precision=highest, preferred_element_type=jnp.float32),
        "shot",
        scatter_dimension=0,
        tiled=True,
    )
    return summed_tiles.reshape(velocity.shape)


def solution(mesh):
    return jax.shard_map(
        shards,
        mesh=mesh,
        in_specs=(
            P(("shot", "sub"), None, None, None),
            P(),
            P(),
            P("shot"),
            P("shot", None),
            P("shot", None),
            P("shot", None, None),
            P("shot", "sub", None, None),
            P("shot", "sub", None, None),
            P("shot", "sub", None, None),
            P("shot", "sub", None, None),
        ),
        out_specs=P(("shot", "sub"), None, None, None),
        check_vma=False,
    )
```

profile of v0, /device:TPU:1, one launch (start us, length us, event | category | flops | bytes accessed | tf_op | source)
XLA Modules:
  0.0 762.4 jit_solution(8612463053049786617)
XLA Ops:
  6.5 2.2 reshape.795
  11.6 56.5 %all-gather.5.cloned.1.call-done = f32[16,2,65536]{2,1,0:T(2,128)} async-done(((f32[1,2,65536]{2,1,0:T(2,128)}), f32[16,2,65536]{2,1,0:T(2,128)}) %all-gather.5.cloned.1.call-update) | async-done | bytes 8388624 | tf_op jit(solution)/shard_map/all_gather | solution.py:57
  68.2 9.7 %reshape.796 = f32[32,65536]{1,0:T(8,128)} reshape(f32[16,2,65536]{2,1,0:T(2,128)} %all-gather.5.cloned.1.call-done) | data formatting | bytes 16777216
  78.0 8.5 %fusion.58 = f32[16,65536]{1,0:T(8,128)} fusion(f32[32,65536]{1,0:T(8,128)} %reshape.796, s32[32]{0:T(128)S(1)} %fusion.62, s32[16]{0:T(128)S(1)} %select_reduce_fusion), kind=kOutput, calls=%fused_computation.251 | convolution fusion | flops 402653696 | bytes 12583104 | tf_op jit(solution)/shard_map/dot_general | solution.py:64
  86.5 1.3 collective-permute-start.2
  87.8 4.9 collective-permute-start.3
  95.6 204.6 %all-reduce.21.cloned.1.call-done = f32[16,65536]{1,0:T(8,128)} async-done(((f32[16,65536]{1,0:T(8,128)}), f32[16,65536]{1,0:T(8,128)}) %all-reduce.21.cloned.1.call-update) | async-done | bytes 4194320
  300.1 2.4 constant_dynamic-slice_fusion
  305.0 4.9 collective-permute-start.5
  309.9 1.3 collective-permute-start
  311.2 4.9 collective-permute-start.1
  318.8 4.9 collective-permute-start.7
  327.2 5.6 collective-permute-start.9
  335.8 6.1 collective-permute-start.11
  346.0 6.9 collective-permute-start.13
  357.4 7.5 collective-permute-start.15
  368.8 7.3 collective-permute-start.17
  377.3 1.7 gather_fusion.7
  379.0 1.7 gather_fusion.6
  380.8 1.7 gather_fusion.5
  382.5 1.7 gather_fusion.4
  384.2 1.7 gather_fusion.3
  386.0 1.7 gather_fusion.2
  387.7 1.7 gather_fusion.1
  390.9 1.7 gather_fusion
  393.3 2.4 scatter_fusion
  395.7 1.3 collective-permute-start.18
  397.0 6.9 collective-permute-start.19
  405.5 2.4 scatter_fusion.1
  407.9 1.3 collective-permute-start.20
  409.2 6.8 collective-permute-start.21
  417.6 2.4 scatter_fusion.2
  421.3 7.0 collective-permute-start.23
  429.9 2.6 scatter_fusion.3
  433.7 6.7 collective-permute-start.25
  442.1 2.4 scatter_fusion.4
  444.5 1.4 collective-permute-start.26
  445.9 7.0 collective-permute-start.27
  454.5 2.4 scatter_fusion.5
  458.2 7.2 collective-permute-start.29
  467.0 2.4 scatter_fusion.6
  470.7 7.4 collective-permute-start.31
  479.7 2.4 scatter_fusion.7
  482.1 2.4 add_multiply_fusion
  484.7 108.1 %all-gather.7.cloned.1.call-done = f32[16,1,65536]{2,1,0:T(1,128)} async-done(((f32[1,1,65536]{2,1,0:T(1,128)}), f32[16,1,65536]{2,1,0:T(1,128)}) %all-gather.7.cloned.1.call-update) | async-done | bytes 4194320 | tf_op jit(solution)/shard_map/all_gather | solution.py:100
  592.9 13.0 %fusion = f32[32,65536]{1,0:T(8,128)} fusion(f32[16,1,65536]{2,1,0:T(1,128)} %all-gather.7.cloned.1.call-done, s32[16]{0:T(128)S(1)} %select_reduce_fusion, s32[32]{0:T(128)S(1)} %copy-done.10), kind=kOutput, calls=%fused_computation.16 | convolution fusion | flops 402653696 | bytes 12583104 | tf_op jit(solution)/shard_map/dot_general | solution.py:110
  607.1 145.9 %all-reduce.23.cloned.1.call-done = f32[32,65536]{1,0:T(8,128)} async-done(((f32[32,65536]{1,0:T(8,128)}), f32[32,65536]{1,0:T(8,128)}) %all-reduce.23.cloned.1.call-update) | async-done | bytes 8388624
  753.0 1.8 dynamic-slice_bitcast_fusion
  (147 shorter events, 45.2 us)
Async XLA Ops:
  6.5 61.6 %all-gather.5.cloned.1.call-start = ((), (), s32[]{:S(2)}) async-start(), calls=%async_computation | async-start | bytes 8912896 | tf_op jit(solution)/shard_map/all_gather | solution.py:57
  8.7 291.4 %all-reduce.21.cloned.1.call-start = ((), (), s32[]{:S(2)}) async-start(), calls=%async_computation.2 | async-start | bytes 8388608
  8.8 69.1 %copy-start.9 = (s32[32]{0:T(128)}, s32[32]{0:T(128)S(1)}, u32[]{:S(2)}) copy-start(s32[32]{0:T(128)S(1)} %fusion.62) | copy-start | bytes 388
  77.9 8.6 %copy-start.2 = (f32[1,8,64,128]{3,2,1,0:T(8,128)S(1)}, f32[1,8,64,128]{3,2,1,0:T(8,128)}, u32[]{:S(2)}) copy-start(f32[1,8,64,128]{3,2,1,0:T(8,128)} %param.35) | copy-start | bytes 786436
  77.9 14.8 %copy-start.6 = (f32[1,8]{1,0:T(1,128)S(1)}, f32[1,8]{1,0:T(1,128)}, u32[]{:S(2)}) copy-start(f32[1,8]{1,0:T(1,128)} %param.31) | copy-start | bytes 100
  77.9 16.2 %copy-start.12 = (u32[256]{0:T(256)S(1)}, u32[256]{0:T(256)}, u32[]{:S(2)}) copy-start(u32[256]{0:T(256)} %constant.251) | copy-start | bytes 3076
  77.9 224.6 %copy-start.5 = (f32[1,8,64,128]{3,2,1,0:T(8,128)S(1)}, f32[1,8,64,128]{3,2,1,0:T(8,128)}, u32[]{:S(2)}) copy-start(f32[1,8,64,128]{3,2,1,0:T(8,128)} %param.34) | copy-start | bytes 786436
  77.9 232.0 %copy-start.3 = (f32[1,8,64,128]{3,2,1,0:T(8,128)S(1)}, f32[1,8,64,128]{3,2,1,0:T(8,128)}, u32[]{:S(2)}) copy-start(f32[1,8,64,128]{3,2,1,0:T(8,128)} %param.37) | copy-start | bytes 786436
  86.4 237.3 %copy-start.7 = (f32[1,8,256]{2,1,0:T(8,128)S(1)}, f32[1,8,256]{2,1,0:T(8,128)}, u32[]{:S(2)}) copy-start(f32[1,8,256]{2,1,0:T(8,128)} %param.33) | copy-start | bytes 24580
  86.5 246.3 %copy-start.8 = (s32[1,256]{1,0:T(1,128)S(1)}, s32[1,256]{1,0:T(1,128)}, u32[]{:S(2)}) copy-start(s32[1,256]{1,0:T(1,128)} %param.32) | copy-start | bytes 3076
  86.5 506.4 %all-gather.7.cloned.1.call-start = ((), (), s32[]{:S(2)}) async-start(), calls=%async_computation.1 | async-start | bytes 4456448 | tf_op jit(solution)/shard_map/all_gather | solution.py:100
  86.5 8.7 %collective-permute-start.2 = (f32[1,64,128]{2,1,0:T(8,128)S(1)}, f32[1,64,128]{2,1,0:T(8,128)S(1)}, u32[]{:S(2)}, u32[]{:S(2)}) collective-permute-start(f32[1,64,128]{2,1,0:T(8,128)S(1)} %get-tuple-element.148), channel_id=1, source_target_pairs={{1,0},{2,1},{3,2},{4,3},{5,4},{6,5},{7,6},{8,7},{9,8},{10,9},{11,1... | collective-permute-start | bytes 98312 | tf_op jit(solution)/shard_map/ppermute | solution.py:15
  87.8 7.4 collective-permute-start.3
  303.7 13.0 %collective-permute-start.4 = (f32[1,64,128]{2,1,0:T(8,128)S(1)}, f32[1,64,128]{2,1,0:T(8,128)S(1)}, u32[]{:S(2)}, u32[]{:S(2)}) collective-permute-start(f32[1,64,128]{2,1,0:T(8,128)S(1)} %get-tuple-element.144), channel_id=1, source_target_pairs={{1,0},{2,1},{3,2},{4,3},{5,4},{6,5},{7,6},{8,7},{9,8},{10,9},{11,1... | collective-permute-start | bytes 98312 | tf_op jit(solution)/shard_map/ppermute | solution.py:15
  305.0 11.7 %collective-permute-start.5 = (f32[1,64,128]{2,1,0:T(8,128)S(1)}, f32[1,64,128]{2,1,0:T(8,128)S(1)}, u32[]{:S(2)}, u32[]{:S(2)}) collective-permute-start(f32[1,64,128]{2,1,0:T(8,128)S(1)} %get-tuple-element.143), channel_id=1, source_target_pairs={{0,1},{1,2},{2,3},{3,4},{4,5},{5,6},{6,7},{7,8},{8,9},{9,10},{10,1... | collective-permute-start | bytes 98312 | tf_op jit(solution)/shard_map/ppermute | solution.py:12
  309.9 55.0 %collective-permute-start = (f32[1,64,128]{2,1,0:T(8,128)S(1)}, f32[1,64,128]{2,1,0:T(8,128)S(1)}, u32[]{:S(2)}, u32[]{:S(2)}) collective-permute-start(f32[1,64,128]{2,1,0:T(8,128)S(1)} %get-tuple-element.146), channel_id=1, source_target_pairs={{1,0},{2,1},{3,2},{4,3},{5,4},{6,5},{7,6},{8,7},{9,8},{10,9},{11,1... | collective-permute-start | bytes 98312 | tf_op jit(solution)/shard_map/ppermute | solution.py:15
  311.2 53.7 %collective-permute-start.1 = (f32[1,64,128]{2,1,0:T(8,128)S(1)}, f32[1,64,128]{2,1,0:T(8,128)S(1)}, u32[]{:S(2)}, u32[]{:S(2)}) collective-permute-start(f32[1,64,128]{2,1,0:T(8,128)S(1)} %get-tuple-element.145), channel_id=1, source_target_pairs={{0,1},{1,2},{2,3},{3,4},{4,5},{5,6},{6,7},{7,8},{8,9},{9,10},{10,1... | collective-permute-start | bytes 98312 | tf_op jit(solution)/shard_map/ppermute | solution.py:12
  317.5 7.5 collective-permute-start.6
  318.8 6.2 collective-permute-start.7
  325.9 7.5 collective-permute-start.8
  327.2 6.6 collective-permute-start.9
  334.5 8.7 %collective-permute-start.10 = (f32[1,64,128]{2,1,0:T(8,128)S(1)}, f32[1,64,128]{2,1,0:T(8,128)S(1)}, u32[]{:S(2)}, u32[]{:S(2)}) collective-permute-start(f32[1,64,128]{2,1,0:T(8,128)S(1)} %get-tuple-element.138), channel_id=1, source_target_pairs={{1,0},{2,1},{3,2},{4,3},{5,4},{6,5},{7,6},{8,7},{9,8},{10,9},{11,1... | collective-permute-start | bytes 98312 | tf_op jit(solution)/shard_map/ppermute | solution.py:15
  335.8 7.4 collective-permute-start.11
  344.7 10.0 %collective-permute-start.12 = (f32[1,64,128]{2,1,0:T(8,128)S(1)}, f32[1,64,128]{2,1,0:T(8,128)S(1)}, u32[]{:S(2)}, u32[]{:S(2)}) collective-permute-start(f32[1,64,128]{2,1,0:T(8,128)S(1)} %get-tuple-element.136), channel_id=1, source_target_pairs={{1,0},{2,1},{3,2},{4,3},{5,4},{6,5},{7,6},{8,7},{9,8},{10,9},{11,1... | collective-permute-start | bytes 98312 | tf_op jit(solution)/shard_map/ppermute | solution.py:15
  346.0 8.7 %collective-permute-start.13 = (f32[1,64,128]{2,1,0:T(8,128)S(1)}, f32[1,64,128]{2,1,0:T(8,128)S(1)}, u32[]{:S(2)}, u32[]{:S(2)}) collective-permute-start(f32[1,64,128]{2,1,0:T(8,128)S(1)} %get-tuple-element.135), channel_id=1, source_target_pairs={{0,1},{1,2},{2,3},{3,4},{4,5},{5,6},{6,7},{7,8},{8,9},{9,10},{10,1... | collective-permute-start | bytes 98312 | tf_op jit(solution)/shard_map/ppermute | solution.py:12
  356.1 9.1 %collective-permute-start.14 = (f32[1,64,128]{2,1,0:T(8,128)S(1)}, f32[1,64,128]{2,1,0:T(8,128)S(1)}, u32[]{:S(2)}, u32[]{:S(2)}) collective-permute-start(f32[1,64,128]{2,1,0:T(8,128)S(1)} %get-tuple-element.134), channel_id=1, source_target_pairs={{1,0},{2,1},{3,2},{4,3},{5,4},{6,5},{7,6},{8,7},{9,8},{10,9},{11,1... | collective-permute-start | bytes 98312 | tf_op jit(solution)/shard_map/ppermute | solution.py:15
  357.4 8.0 %collective-permute-start.15 = (f32[1,64,128]{2,1,0:T(8,128)S(1)}, f32[1,64,128]{2,1,0:T(8,128)S(1)}, u32[]{:S(2)}, u32[]{:S(2)}) collective-permute-start(f32[1,64,128]{2,1,0:T(8,128)S(1)} %get-tuple-element.133), channel_id=1, source_target_pairs={{0,1},{1,2},{2,3},{3,4},{4,5},{5,6},{6,7},{7,8},{8,9},{9,10},{10,1... | collective-permute-start | bytes 98312 | tf_op jit(solution)/shard_map/ppermute | solution.py:12
  367.5 21.9 %collective-permute-start.16 = (f32[1,64,128]{2,1,0:T(8,128)}, f32[1,64,128]{2,1,0:T(8,128)S(1)}, u32[]{:S(2)}, u32[]{:S(2)}) collective-permute-start(f32[1,64,128]{2,1,0:T(8,128)} %get-tuple-element.132), channel_id=1, source_target_pairs={{1,0},{2,1},{3,2},{4,3},{5,4},{6,5},{7,6},{8,7},{9,8},{10,9},{11,1... | collective-permute-start | bytes 98312 | tf_op jit(solution)/shard_map/ppermute | solution.py:15
  368.8 20.7 %collective-permute-start.17 = (f32[1,64,128]{2,1,0:T(8,128)}, f32[1,64,128]{2,1,0:T(8,128)S(1)}, u32[]{:S(2)}, u32[]{:S(2)}) collective-permute-start(f32[1,64,128]{2,1,0:T(8,128)} %get-tuple-element.131), channel_id=1, source_target_pairs={{0,1},{1,2},{2,3},{3,4},{4,5},{5,6},{6,7},{7,8},{8,9},{9,10},{10,1... | collective-permute-start | bytes 98312 | tf_op jit(solution)/shard_map/ppermute | solution.py:12
  395.7 8.2 %collective-permute-start.18 = (f32[1,64,128]{2,1,0:T(8,128)S(1)}, f32[1,64,128]{2,1,0:T(8,128)S(1)}, u32[]{:S(2)}, u32[]{:S(2)}) collective-permute-start(f32[1,64,128]{2,1,0:T(8,128)S(1)} %get-tuple-element.130), channel_id=1, source_target_pairs={{1,0},{2,1},{3,2},{4,3},{5,4},{6,5},{7,6},{8,7},{9,8},{10,9},{11,1... | collective-permute-start | bytes 98312 | tf_op jit(solution)/shard_map/ppermute | solution.py:15
  397.0 7.9 %collective-permute-start.19 = (f32[1,64,128]{2,1,0:T(8,128)S(1)}, f32[1,64,128]{2,1,0:T(8,128)S(1)}, u32[]{:S(2)}, u32[]{:S(2)}) collective-permute-start(f32[1,64,128]{2,1,0:T(8,128)S(1)} %get-tuple-element.129), channel_id=1, source_target_pairs={{0,1},{1,2},{2,3},{3,4},{4,5},{5,6},{6,7},{7,8},{8,9},{9,10},{10,1... | collective-permute-start | bytes 98312 | tf_op jit(solution)/shard_map/ppermute | solution.py:12
  407.9 8.1 %collective-permute-start.20 = (f32[1,64,128]{2,1,0:T(8,128)S(1)}, f32[1,64,128]{2,1,0:T(8,128)S(1)}, u32[]{:S(2)}, u32[]{:S(2)}) collective-permute-start(f32[1,64,128]{2,1,0:T(8,128)S(1)} %get-tuple-element.128), channel_id=1, source_target_pairs={{1,0},{2,1},{3,2},{4,3},{5,4},{6,5},{7,6},{8,7},{9,8},{10,9},{11,1... | collective-permute-start | bytes 98312 | tf_op jit(solution)/shard_map/ppermute | solution.py:15
  409.2 7.8 %collective-permute-start.21 = (f32[1,64,128]{2,1,0:T(8,128)S(1)}, f32[1,64,128]{2,1,0:T(8,128)S(1)}, u32[]{:S(2)}, u32[]{:S(2)}) collective-permute-start(f32[1,64,128]{2,1,0:T(8,128)S(1)} %get-tuple-element.127), channel_id=1, source_target_pairs={{0,1},{1,2},{2,3},{3,4},{4,5},{5,6},{6,7},{7,8},{8,9},{9,10},{10,1... | collective-permute-start | bytes 98312 | tf_op jit(solution)/shard_map/ppermute | solution.py:12
  420.0 8.3 %collective-permute-start.22 = (f32[1,64,128]{2,1,0:T(8,128)S(1)}, f32[1,64,128]{2,1,0:T(8,128)S(1)}, u32[]{:S(2)}, u32[]{:S(2)}) collective-permute-start(f32[1,64,128]{2,1,0:T(8,128)S(1)} %get-tuple-element.126), channel_id=1, source_target_pairs={{1,0},{2,1},{3,2},{4,3},{5,4},{6,5},{7,6},{8,7},{9,8},{10,9},{11,1... | collective-permute-start | bytes 98312 | tf_op jit(solution)/shard_map/ppermute | solution.py:15
  421.3 8.0 %collective-permute-start.23 = (f32[1,64,128]{2,1,0:T(8,128)S(1)}, f32[1,64,128]{2,1,0:T(8,128)S(1)}, u32[]{:S(2)}, u32[]{:S(2)}) collective-permute-start(f32[1,64,128]{2,1,0:T(8,128)S(1)} %get-tuple-element.125), channel_id=1, source_target_pairs={{0,1},{1,2},{2,3},{3,4},{4,5},{5,6},{6,7},{7,8},{8,9},{9,10},{10,1... | collective-permute-start | bytes 98312 | tf_op jit(solution)/shard_map/ppermute | solution.py:12
  432.4 8.2 %collective-permute-start.24 = (f32[1,64,128]{2,1,0:T(8,128)S(1)}, f32[1,64,128]{2,1,0:T(8,128)S(1)}, u32[]{:S(2)}, u32[]{:S(2)}) collective-permute-start(f32[1,64,128]{2,1,0:T(8,128)S(1)} %get-tuple-element.124), channel_id=1, source_target_pairs={{1,0},{2,1},{3,2},{4,3},{5,4},{6,5},{7,6},{8,7},{9,8},{10,9},{11,1... | collective-permute-start | bytes 98312 | tf_op jit(solution)/shard_map/ppermute | solution.py:15
  433.7 7.8 %collective-permute-start.25 = (f32[1,64,128]{2,1,0:T(8,128)S(1)}, f32[1,64,128]{2,1,0:T(8,128)S(1)}, u32[]{:S(2)}, u32[]{:S(2)}) collective-permute-start(f32[1,64,128]{2,1,0:T(8,128)S(1)} %get-tuple-element.123), channel_id=1, source_target_pairs={{0,1},{1,2},{2,3},{3,4},{4,5},{5,6},{6,7},{7,8},{8,9},{9,10},{10,1... | collective-permute-start | bytes 98312 | tf_op jit(solution)/shard_map/ppermute | solution.py:12
  444.5 37.6 %copy-start.4 = (f32[8,64,128]{2,1,0:T(8,128)S(1)}, f32[8,64,128]{2,1,0:T(8,128)}, u32[]{:S(2)}) copy-start(f32[8,64,128]{2,1,0:T(8,128)} %get-tuple-element.108) | copy-start | bytes 786436
  444.5 8.4 %collective-permute-start.26 = (f32[1,64,128]{2,1,0:T(8,128)S(1)}, f32[1,64,128]{2,1,0:T(8,128)S(1)}, u32[]{:S(2)}, u32[]{:S(2)}) collective-permute-start(f32[1,64,128]{2,1,0:T(8,128)S(1)} %get-tuple-element.122), channel_id=1, source_target_pairs={{1,0},{2,1},{3,2},{4,3},{5,4},{6,5},{7,6},{8,7},{9,8},{10,9},{11,1... | collective-permute-start | bytes 98312 | tf_op jit(solution)/shard_map/ppermute | solution.py:15
  445.9 8.0 %collective-permute-start.27 = (f32[1,64,128]{2,1,0:T(8,128)S(1)}, f32[1,64,128]{2,1,0:T(8,128)S(1)}, u32[]{:S(2)}, u32[]{:S(2)}) collective-permute-start(f32[1,64,128]{2,1,0:T(8,128)S(1)} %get-tuple-element.121), channel_id=1, source_target_pairs={{0,1},{1,2},{2,3},{3,4},{4,5},{5,6},{6,7},{7,8},{8,9},{9,10},{10,1... | collective-permute-start | bytes 98312 | tf_op jit(solution)/shard_map/ppermute | solution.py:12
  456.9 136.0 %copy-start.10 = (s32[32]{0:T(128)S(1)}, s32[32]{0:T(128)}, u32[]{:S(2)}) copy-start(s32[32]{0:T(128)} %copy-done.9) | copy-start | bytes 388
  456.9 8.5 %collective-permute-start.28 = (f32[1,64,128]{2,1,0:T(8,128)S(1)}, f32[1,64,128]{2,1,0:T(8,128)S(1)}, u32[]{:S(2)}, u32[]{:S(2)}) collective-permute-start(f32[1,64,128]{2,1,0:T(8,128)S(1)} %get-tuple-element.120), channel_id=1, source_target_pairs={{1,0},{2,1},{3,2},{4,3},{5,4},{6,5},{7,6},{8,7},{9,8},{10,9},{11,1... | collective-permute-start | bytes 98312 | tf_op jit(solution)/shard_map/ppermute | solution.py:15
  458.2 8.2 %collective-permute-start.29 = (f32[1,64,128]{2,1,0:T(8,128)S(1)}, f32[1,64,128]{2,1,0:T(8,128)S(1)}, u32[]{:S(2)}, u32[]{:S(2)}) collective-permute-start(f32[1,64,128]{2,1,0:T(8,128)S(1)} %get-tuple-element.119), channel_id=1, source_target_pairs={{0,1},{1,2},{2,3},{3,4},{4,5},{5,6},{6,7},{7,8},{8,9},{9,10},{10,1... | collective-permute-start | bytes 98312 | tf_op jit(solution)/shard_map/ppermute | solution.py:12
  469.4 8.7 %collective-permute-start.30 = (f32[1,64,128]{2,1,0:T(8,128)S(1)}, f32[1,64,128]{2,1,0:T(8,128)S(1)}, u32[]{:S(2)}, u32[]{:S(2)}) collective-permute-start(f32[1,64,128]{2,1,0:T(8,128)S(1)} %get-tuple-element.118), channel_id=1, source_target_pairs={{1,0},{2,1},{3,2},{4,3},{5,4},{6,5},{7,6},{8,7},{9,8},{10,9},{11,1... | collective-permute-start | bytes 98312 | tf_op jit(solution)/shard_map/ppermute | solution.py:15
  470.7 8.4 %collective-permute-start.31 = (f32[1,64,128]{2,1,0:T(8,128)S(1)}, f32[1,64,128]{2,1,0:T(8,128)S(1)}, u32[]{:S(2)}, u32[]{:S(2)}) collective-permute-start(f32[1,64,128]{2,1,0:T(8,128)S(1)} %get-tuple-element.117), channel_id=1, source_target_pairs={{0,1},{1,2},{2,3},{3,4},{4,5},{5,6},{6,7},{7,8},{8,9},{9,10},{10,1... | collective-permute-start | bytes 98312 | tf_op jit(solution)/shard_map/ppermute | solution.py:12
  484.4 121.4 %copy-start.11 = (u32[256]{0:T(256)S(1)}, u32[256]{0:T(256)}, u32[]{:S(2)}) copy-start(u32[256]{0:T(256)} %constant.255) | copy-start | bytes 3076
  484.5 268.5 %all-reduce.23.cloned.1.call-start = ((), (), s32[]{:S(2)}) async-start(), calls=%async_computation.3 | async-start | bytes 16777216
  592.9 162.8 %copy-start.1 = (s32[16,2]{0,1:T(2,128)S(1)}, s32[16,2]{0,1:T(2,128)}, u32[]{:S(2)}) copy-start(s32[16,2]{0,1:T(2,128)} %param.29) | copy-start | bytes 388
  (1 other events, 2.3 us)
Sparse Core Ops, SparseCore 0:
  9.2 58.9 all-gather.4
  86.6 213.4 all-reduce.20
  484.6 108.2 all-gather.6
  606.0 146.9 all-reduce.22
where the time goes:
time: 772 us; the launch traced here: 762 us
  waiting for transfers between devices  523 us (68%)
  starting transfers between devices  123 us (16%)
  other arithmetic  39.8 us (5%)
  local copies, waits for them, and re-layouts  34.6 us (4%)
  matrix products  21.5 us (3%)
  between operations  20.6 us (3%)
    unnamed x6, waiting for transfers between devices  351 us
    all_gather x1, waiting for transfers between devices, shards(): group_grads = lax.all_gather(shot_gradient, 'sub', axis=0, tiled=True)  108 us
    ppermute x16, starting transfers between devices, padded_2(): lax.ppermute(lax.slice_in_dim(block, block.shape[dim] - width, None, axis...  102 us
    all_gather x1, waiting for transfers between devices, shards(): gathered = lax.all_gather(flat_vel, 'shot', axis=0, tiled=True)  56.5 us
    ppermute x16, starting transfers between devices, padded_2(): lax.ppermute(lax.slice_in_dim(block, 0, width, axis=dim), axis, backward)  20.8 us
    scatter-add x8, other arithmetic, shards(): advanced = advanced.reshape(-1).at[rec_index].add(residuals[step_count -...  19.3 us
    unnamed x33, local copies, waits for them, and re-layouts  18.1 us
  transfers between devices with their start and end apart: 36, of which 14 were waited for; matrix products, arithmetic and copies ran while one was open for 3% of the time, Pallas kernels for 0%

commit v1 on v0

v1 whole, which is shorter than its diff:
```python
import jax
import jax.numpy as jnp
from jax import lax
from jax.experimental import pallas as pl
from jax.experimental.pallas import tpu as pltpu
from jax.sharding import PartitionSpec as P

ALL = ("shot", "sub")
LANES = 128
STEPS = 8
REC = 256
T = 8
PADY = 8


def split3(x):
    hi = x.astype(jnp.bfloat16)
    rest = x - hi.astype(jnp.float32)
    mid = rest.astype(jnp.bfloat16)
    lo = (rest - mid.astype(jnp.float32)).astype(jnp.bfloat16)
    return hi, mid, lo


def dot3(onehot, x, dims):
    total = None
    for part in reversed(split3(x)):
        term = lax.dot_general(onehot, part, (dims, ((), ())), preferred_element_type=jnp.float32)
        total = term if total is None else total + term
    return total


def pick_kernel(index_ref, x_ref, out_ref):
    rows = x_ref.shape[0]
    index = index_ref[...]
    onehot = (lax.broadcasted_iota(jnp.int32, (rows, index.shape[1]), 0) == index).astype(jnp.bfloat16)
    out_ref[...] = dot3(onehot, x_ref[...], ((0,), (0,)))


def drop_kernel(index_ref, x_ref, out_ref):
    rows = out_ref.shape[0]
    index = index_ref[...]
    onehot = (lax.broadcasted_iota(jnp.int32, (rows, index.shape[1]), 0) == index).astype(jnp.bfloat16)
    out_ref[...] = dot3(onehot, x_ref[...], ((1,), (0,)))


def load_field(dst, low, own, high):
    ny = own.shape[1]
    for block, ref in enumerate((low, own, high)):
        dst[block * T : (block + 1) * T, PADY : PADY + ny, :] = ref[...]


def clear_pad(dst, ny):
    zero = jnp.zeros((dst.shape[0], PADY, LANES), jnp.float32)
    dst[:, 0:PADY, :] = zero
    dst[:, PADY + ny : PADY + ny + PADY, :] = zero


def layer_laplace(cur, x, ny, first, last):
    mid = cur[x, PADY : PADY + ny, :]
    total = cur[x + 1, PADY : PADY + ny, :] + cur[x - 1, PADY : PADY + ny, :]
    total = total + cur[x, PADY + 1 : PADY + 1 + ny, :] + cur[x, PADY - 1 : PADY - 1 + ny, :]
    up = jnp.where(last, 0.0, pltpu.roll(mid, LANES - 1, 1))
    down = jnp.where(first, 0.0, pltpu.roll(mid, 1, 1))
    total = total + up + down
    return mid, total - 6.0 * mid


def forward_kernel(
    src_ref, wave_ref, rec_ref, obs_ref,
    sl, so, sh, pl_, po, ph, cl, co, ch,
    lap_ref, res_ref, prev, cur, speed_sq,
):
    ny = so.shape[1]
    rows = T * ny
    clear_pad(prev, ny)
    clear_pad(cur, ny)
    load_field(prev, pl_, po, ph)
    load_field(cur, cl, co, ch)
    for block, ref in enumerate((sl, so, sh)):
        value = ref[...]
        speed_sq[block * T : (block + 1) * T] = value * value
    lane = lax.broadcasted_iota(jnp.int32, (ny, LANES), 1)
    first, last = lane == 0, lane == LANES - 1
    src_x, src_y, src_z = src_ref[0], src_ref[1], src_ref[2]
    inside = (src_x >= 0) & (src_x < 3 * T)
    src_lane = lax.broadcasted_iota(jnp.int32, (1, LANES), 1) == src_z
    rec = rec_ref[...]
    onehot = (lax.broadcasted_iota(jnp.int32, (rows, REC), 0) == rec[0:1]).astype(jnp.bfloat16)
    z_mask = lax.broadcasted_iota(jnp.int32, (LANES, REC), 0) == rec[1:2]
    own = (rec[0:1] >= 0) & (rec[0:1] < rows)
    for n in range(STEPS):
        old, now = (prev, cur) if n % 2 == 0 else (cur, prev)

        def update(x, keep):
            mid, lap = layer_laplace(now, x, ny, first, last)
            old[x, PADY : PADY + ny, :] = (2.0 * mid - old[x, PADY : PADY + ny, :]) + speed_sq[x] * lap
            return lap

        def outer(x, carry):
            update(x, False)
            return carry

        def inner(x, carry):
            lap_ref[n, x - T] = update(x, True)
            return carry

        lax.fori_loop(1 + n, T, outer, 0)
        lax.fori_loop(T, 2 * T, inner, 0)
        lax.fori_loop(2 * T, 3 * T - 1 - n, outer, 0)

        @pl.when(inside)
        def _():
            row = pl.ds(src_y + PADY, 1)
            old[src_x, row, :] = old[src_x, row, :] + jnp.where(src_lane, wave_ref[n], 0.0)

        field = old[T : 2 * T, PADY : PADY + ny, :].reshape(rows, LANES)
        total = None
        for part in reversed(split3(field)):
            term = lax.dot_general(part, onehot, (((0,), (0,)), ((), ())), preferred_element_type=jnp.float32)
            total = term if total is None else total + term
        sample = jnp.sum(jnp.where(z_mask, total, 0.0), axis=0, keepdims=True)
        res_ref[n : n + 1, :] = jnp.where(own, sample - obs_ref[n : n + 1, :], 0.0)


def adjoint_kernel(
    rec_ref, rl, ro, rh,
    sl, so, sh, pl_, po, ph, cl, co, ch, lap_ref,
    out_ref, prev, cur, speed_sq, inject,
):
    ny = so.shape[1]
    clear_pad(prev, ny)
    clear_pad(cur, ny)
    load_field(prev, pl_, po, ph)
    load_field(cur, cl, co, ch)
    for block, ref in enumerate((sl, so, sh)):
        value = ref[...]
        speed_sq[block * T : (block + 1) * T] = value * value
    lane = lax.broadcasted_iota(jnp.int32, (ny, LANES), 1)
    first, last = lane == 0, lane == LANES - 1
    rec = rec_ref[...]
    resid = rl[...] + ro[...] + rh[...]
    z_mask = lax.broadcasted_iota(jnp.int32, (LANES, REC), 0) == rec[1:2]
    for k in range(STEPS):
        old, now = (prev, cur) if k % 2 == 0 else (cur, prev)
        n = STEPS - 1 - k
        lo, hi = 1 + k, 3 * T - 1 - k
        span = (hi - lo) * ny
        onehot = (
            lax.broadcasted_iota(jnp.int32, (span, REC), 0) == rec[0:1] + (T - lo) * ny
        ).astype(jnp.bfloat16)
        spread = jnp.where(z_mask, resid[n : n + 1, :], 0.0)
        inject[lo:hi] = dot3(onehot, spread, ((1,), (1,))).reshape(hi - lo, ny, LANES)

        def update(x):
            mid, lap = layer_laplace(now, x, ny, first, last)
            new = (2.0 * mid - old[x, PADY : PADY + ny, :]) + speed_sq[x] * lap + inject[x]
            old[x, PADY : PADY + ny, :] = new
            return new

        def outer(x, carry):
            update(x)
            return carry

        def inner(x, carry):
            new = update(x)
            term = so[x - T] * new * lap_ref[n, x - T]
            if k == 0:
                out_ref[x - T] = term
            elif k == STEPS - 1:
                out_ref[x - T] = (2.0 / STEPS) * (out_ref[x - T] + term)
            else:
                out_ref[x - T] = out_ref[x - T] + term
            return carry

        lax.fori_loop(lo, T, outer, 0)
        lax.fori_loop(T, 2 * T, inner, 0)
        lax.fori_loop(2 * T, hi, outer, 0)


def vmem():
    return pl.BlockSpec(memory_space=pltpu.VMEM)


def smem():
    return pl.BlockSpec(memory_space=pltpu.SMEM)


def params():
    return pltpu.CompilerParams(vmem_limit_bytes=48 * 1024 * 1024)


def shards(
    velocity,
    tile_slot,
    anchors,
    source_cell,
    wavelet,
    receiver_cells,
    observed,
    fwd_prev,
    fwd_curr,
    adj_prev,
    adj_curr,
):
    n_shot = lax.axis_size("shot")
    n_sub = lax.axis_size("sub")
    n_all = n_shot * n_sub
    sub_index = lax.axis_index("sub")
    local_slots, layers, ny, nz = velocity.shape
    rows = layers * ny
    piece = rows // n_all
    forward = [(i, i + 1) for i in range(n_sub - 1)]
    backward = [(j, i) for i, j in forward]

    def both(x):
        return lax.ppermute(x, "sub", forward), lax.ppermute(x, "sub", backward)

    tiles = ((anchors[:, 0:1] + jnp.arange(n_sub, dtype=jnp.int32)) * n_shot + anchors[:, 1:2]).reshape(-1)
    table = jnp.arange(tile_slot.shape[0], dtype=jnp.int32)
    wanted = jnp.sum(jnp.where(table[:, None] == tiles[None, :], tile_slot[:, None], 0), axis=0)
    want_rows = (wanted[:, None] * piece + jnp.arange(piece, dtype=jnp.int32)).reshape(1, n_all * piece)

    cells = receiver_cells[0]
    rec = jnp.stack([cells // nz - sub_index * rows, cells % nz])
    src = source_cell[0]
    src_place = jnp.stack([src // (ny * nz) - (sub_index - 1) * layers, src // nz % ny, src % nz])

    with jax.named_scope("spread_velocity"):
        cut = velocity.reshape(local_slots, n_all, piece, nz).transpose(1, 0, 2, 3)
        spread = lax.all_to_all(cut.reshape(n_all, local_slots * piece, nz), ALL, 0, 0, tiled=True)
    with jax.named_scope("pick_velocity"):
        picked = pl.pallas_call(
            pick_kernel,
            out_shape=jax.ShapeDtypeStruct((n_all * piece, nz), jnp.float32),
            in_specs=[vmem(), vmem()],
            out_specs=vmem(),
            compiler_params=params(),
        )(want_rows, spread.reshape(n_all * local_slots * piece, nz))
    with jax.named_scope("deliver_velocity"):
        speed = lax.all_to_all(picked.reshape(n_all, piece, nz), ALL, 0, 0, tiled=True).reshape(layers, ny, nz)

    def triple(x):
        low, high = both(x)
        return low, x, high

    with jax.named_scope("halo_fwd"):
        prev3, cur3 = triple(fwd_prev[0]), triple(fwd_curr[0])
    with jax.named_scope("halo_adj"):
        aprev3, acur3 = triple(adj_prev[0]), triple(adj_curr[0])
    with jax.named_scope("halo_speed"):
        speed3 = triple(speed)

    field = pltpu.VMEM((3 * T, ny + 2 * PADY, nz), jnp.float32)
    flat = pltpu.VMEM((3 * T, ny, nz), jnp.float32)
    with jax.named_scope("forward"):
        laps, resid = pl.pallas_call(
            forward_kernel,
            out_shape=(
                jax.ShapeDtypeStruct((STEPS, layers, ny, nz), jnp.float32),
                jax.ShapeDtypeStruct((STEPS, REC), jnp.float32),
            ),
            in_specs=[smem(), smem()] + [vmem()] * 11,
            out_specs=(vmem(), vmem()),
            scratch_shapes=[field, field, flat],
            compiler_params=params(),
        )(src_place, wavelet[0], rec, observed[0], *speed3, *prev3, *cur3)
    with jax.named_scope("residuals"):
        res3 = triple(resid)
    with jax.named_scope("adjoint"):
        image = pl.pallas_call(
            adjoint_kernel,
            out_shape=jax.ShapeDtypeStruct((layers, ny, nz), jnp.float32),
            in_specs=[vmem()] * 14,
            out_specs=vmem(),
            scratch_shapes=[field, field, flat, flat],
            compiler_params=params(),
        )(rec, *res3, *speed3, *aprev3, *acur3, laps)

    with jax.named_scope("spread_gradient"):
        pieces = lax.all_to_all(image.reshape(n_all, piece, nz), ALL, 0, 0, tiled=True)
    with jax.named_scope("drop_gradient"):
        dropped = pl.pallas_call(
            drop_kernel,
            out_shape=jax.ShapeDtypeStruct((n_all * local_slots * piece, nz), jnp.float32),
            in_specs=[vmem(), vmem()],
            out_specs=vmem(),
            compiler_params=params(),
        )(want_rows, pieces.reshape(n_all * piece, nz))
    with jax.named_scope("deliver_gradient"):
        back = lax.all_to_all(dropped.reshape(n_all, local_slots * piece, nz), ALL, 0, 0, tiled=True)
        back = back.reshape(n_all, local_slots, piece, nz).transpose(1, 0, 2, 3)
    return back.reshape(velocity.shape)


def solution(mesh):
    return jax.shard_map(
        shards,
        mesh=mesh,
        in_specs=(
            P(("shot", "sub"), None, None, None),
            P(),
            P(),
            P("shot"),
            P("shot", None),
            P("shot", None),
            P("shot", None, None),
            P("shot", "sub", None, None),
            P("shot", "sub", None, None),
            P("shot", "sub", None, None),
            P("shot", "sub", None, None),
        ),
        out_specs=P(("shot", "sub"), None, None, None),
        check_vma=False,
    )
```

time: 772 us -> 217 us (0.28); the launches traced: 762 us -> 216 us
  waiting for transfers between devices: 523 us -> 54.7 us
  starting transfers between devices: 123 us -> 61.5 us
  blocking collectives: 0 us -> 57.3 us
  other arithmetic: 39.8 us -> 0.43 us
  Pallas kernels: 0 us -> 37.6 us
  local copies, waits for them, and re-layouts: 34.6 us -> 3.33 us
  matrix products: 21.5 us -> 0 us
  between operations: 20.6 us -> 1.03 us
    unnamed x6 -> x0, waiting for transfers between devices: 351 us -> none
    all_gather x2 -> x0, waiting for transfers between devices: 165 us -> none  [the longest x1 108 us: shards(): group_grads = lax.all_gather(shot_gradient, 'sub', axis=0, tiled=True)]
    ppermute x32 -> x12, starting transfers between devices: 123 us -> 40.7 us  [both(): return (lax.ppermute(x, 'sub', forward), lax.ppermute(x, 'sub', backward))]
    all_to_all x0 -> x2, blocking collectives: none -> 57.3 us  [the longest x1 31.2 us: shards(): lax.all_to_all(image.reshape(n_all, piece, nz), ALL, 0, 0, tiled=True)]
    pallas_call x0 -> x4, Pallas kernels: none -> 37.6 us  [the longest x1 19.9 us: shards(): pl.pallas_call(adjoint_kernel, out_shape=jax.ShapeDtypeStruct((layers, ny...]
    ppermute x32 -> x12, waiting for transfers between devices: 7.63 us -> 32.5 us  [both(): return (lax.ppermute(x, 'sub', forward), lax.ppermute(x, 'sub', backward))]
    all_to_all x0 -> x2, waiting for transfers between devices: none -> 22.3 us  [the longest x1 20.3 us: shards(): lax.all_to_all(cut.reshape(n_all, local_slots * piece, nz), ALL, 0, 0, ti...]
    dot_general x2 -> x0, matrix products: 21.5 us -> none  [the longest x1 13 us: shards(): jnp.dot(picker, group_grads, precision=highest, preferred_element_type=jn...]
  transfers between devices with their start and end apart: 36 -> 14, of which waited for: 14 -> 5; matrix products, arithmetic and copies ran while one was open for 3% -> 0% of each run, Pallas kernels for 0% -> 7%
where the time goes in v1:
time: 217 us; the launch traced here: 216 us
  starting transfers between devices  61.5 us (28%)
  blocking collectives  57.3 us (26%)
  waiting for transfers between devices  54.7 us (25%)
  Pallas kernels  37.6 us (17%)
  local copies, waits for them, and re-layouts  3.33 us (2%)
    ppermute x12, starting transfers between devices, both(): return (lax.ppermute(x, 'sub', forward), lax.ppermute(x, 'sub', backward))  40.7 us
    ppermute x12, waiting for transfers between devices, both(): return (lax.ppermute(x, 'sub', forward), lax.ppermute(x, 'sub', backward))  32.5 us
    all_to_all x1, blocking collectives, shards(): lax.all_to_all(image.reshape(n_all, piece, nz), ALL, 0, 0, tiled=True)  31.2 us
    all_to_all x1, blocking collectives, shards(): lax.all_to_all(dropped.reshape(n_all, local_slots * piece, nz), ALL, 0, 0...  26.1 us
    all_to_all x1, waiting for transfers between devices, shards(): lax.all_to_all(cut.reshape(n_all, local_slots * piece, nz), ALL, 0, 0, ti...  20.3 us
    pallas_call x1, Pallas kernels, shards(): pl.pallas_call(adjoint_kernel, out_shape=jax.ShapeDtypeStruct((layers, ny...  19.9 us
    all_to_all x1, starting transfers between devices, shards(): lax.all_to_all(cut.reshape(n_all, local_slots * piece, nz), ALL, 0, 0, ti...  15.7 us
    pallas_call x1, Pallas kernels, shards(): pl.pallas_call(forward_kernel, out_shape=(jax.ShapeDtypeStruct((STEPS, la...  14.9 us
  transfers between devices with their start and end apart: 14, of which 5 were waited for; matrix products, arithmetic and copies ran while one was open for 0% of the time, Pallas kernels for 7%

profile of v1, /device:TPU:1, one launch (start us, length us, event | category | flops | bytes accessed | tf_op | source)
XLA Modules:
  0.0 215.9 jit_solution(10230793835311401821)
XLA Ops:
  0.0 0.0 copy-start.1
  0.0 0.0 copy-start.3
  0.0 0.0 copy-start.2
  0.0 0.0 copy-start.7
  0.0 0.0 copy-start.5
  0.1 0.0 copy-start.4
  0.1 2.1 copy.16
  2.2 15.7 %all-to-all-start = ((f32[256,4,128]{2,1,0:T(4,128)}), f32[256,4,128]{2,1,0:T(4,128)S(1)}, u32[]{:S(2)}, u32[]{:S(2)}) async-start(f32[256,4,128]{2,1,0:T(4,128)} %bitcast.10), calls=%async_computation | async-start | bytes 1048576 | tf_op jit(solution)/shard_map/spread_velocity/all_to_all | solution.py:230
  17.9 0.1 multiply_add_fusion
  17.9 0.1 add.86
  18.0 0.2 select_reduce_fusion
  18.2 0.1 iota_add_fusion
  18.3 0.1 add.90.index_ref
  18.4 20.3 %all-to-all-done = f32[256,4,128]{2,1,0:T(4,128)S(1)} async-done(((f32[256,4,128]{2,1,0:T(4,128)}), f32[256,4,128]{2,1,0:T(4,128)S(1)}, u32[]{:S(2)}, u32[]{:S(2)}) %all-to-all-start) | async-done | bytes 524320 | tf_op jit(solution)/shard_map/spread_velocity/all_to_all | solution.py:230
  38.7 1.8 pick_velocity.1
  40.5 5.2 %all-to-all-start.1 = ((f32[256,2,128]{2,1,0:T(2,128)}), f32[256,2,128]{2,1,0:T(2,128)S(1)}, u32[]{:S(2)}, u32[]{:S(2)}) async-start(f32[256,2,128]{2,1,0:T(2,128)} %bitcast.12), calls=%async_computation.1 | async-start | bytes 524288 | tf_op jit(solution)/shard_map/deliver_velocity/all_to_all | solution.py:240
  45.7 4.4 %collective-permute-start.2 = (f32[8,64,128]{2,1,0:T(8,128)S(1)}, f32[8,64,128]{2,1,0:T(8,128)S(1)}, u32[]{:S(2)}, u32[]{:S(2)}) collective-permute-start(f32[8,64,128]{2,1,0:T(8,128)S(1)} %bitcast.40), channel_id=1, source_target_pairs={{0,1},{1,2},{2,3},{3,4},{4,5},{5,6},{6,7},{7,8},{8,9},{9,10},{10,1... | collective-permute-start | bytes 786440 | tf_op jit(solution)/shard_map/halo_fwd/ppermute | solution.py:216
  50.1 1.3 collective-permute-start.3
  51.4 6.4 %collective-permute-start.4 = (f32[8,64,128]{2,1,0:T(8,128)S(1)}, f32[8,64,128]{2,1,0:T(8,128)S(1)}, u32[]{:S(2)}, u32[]{:S(2)}) collective-permute-start(f32[8,64,128]{2,1,0:T(8,128)S(1)} %bitcast.43), channel_id=1, source_target_pairs={{0,1},{1,2},{2,3},{3,4},{4,5},{5,6},{6,7},{7,8},{8,9},{9,10},{10,1... | collective-permute-start | bytes 786440 | tf_op jit(solution)/shard_map/halo_fwd/ppermute | solution.py:216
  57.8 1.3 collective-permute-start.5
  59.1 2.0 all-to-all-done.1
  61.1 4.2 %collective-permute-start = (f32[8,64,128]{2,1,0:T(8,128)S(1)}, f32[8,64,128]{2,1,0:T(8,128)S(1)}, u32[]{:S(2)}, u32[]{:S(2)}) collective-permute-start(f32[8,64,128]{2,1,0:T(8,128)S(1)} %bitcast.32), channel_id=1, source_target_pairs={{0,1},{1,2},{2,3},{3,4},{4,5},{5,6},{6,7},{7,8},{8,9},{9,10},{10,1... | collective-permute-start | bytes 786440 | tf_op jit(solution)/shard_map/halo_speed/ppermute | solution.py:216
  65.2 0.0 collective-permute-done.2.pl_
  65.2 5.5 %collective-permute-start.10 = (f32[8,64,128]{2,1,0:T(8,128)S(1)}, f32[8,64,128]{2,1,0:T(8,128)S(1)}, u32[]{:S(2)}, u32[]{:S(2)}) collective-permute-start(f32[8,64,128]{2,1,0:T(8,128)S(1)} %bitcast.49), channel_id=1, source_target_pairs={{0,1},{1,2},{2,3},{3,4},{4,5},{5,6},{6,7},{7,8},{8,9},{9,10},{10,1... | collective-permute-start | bytes 786440 | tf_op jit(solution)/shard_map/halo_adj/ppermute | solution.py:216
  70.7 3.0 %collective-permute-done.3.ph = f32[8,64,128]{2,1,0:T(8,128)S(1)} collective-permute-done((f32[8,64,128]{2,1,0:T(8,128)S(1)}, f32[8,64,128]{2,1,0:T(8,128)S(1)}, u32[]{:S(2)}, u32[]{:S(2)}) %collective-permute-start.3) | collective-permute-done | bytes 262176 | tf_op jit(solution)/shard_map/halo_fwd/ppermute | solution.py:216
  73.7 1.3 collective-permute-start.11
  75.0 0.0 collective-permute-done.4.cl
  75.0 5.6 %collective-permute-start.8 = (f32[8,64,128]{2,1,0:T(8,128)S(1)}, f32[8,64,128]{2,1,0:T(8,128)}, u32[]{:S(2)}, u32[]{:S(2)}) collective-permute-start(f32[8,64,128]{2,1,0:T(8,128)S(1)} %bitcast.46), channel_id=1, source_target_pairs={{0,1},{1,2},{2,3},{3,4},{4,5},{5,6},{6,7},{7,8},{8,9},{9,10},{10,1... | collective-permute-start | bytes 786440 | tf_op jit(solution)/shard_map/halo_adj/ppermute | solution.py:216
  80.6 0.0 collective-permute-done.5.ch
  80.6 1.3 collective-permute-start.9
  81.9 0.0 collective-permute-done.sl
  81.9 1.3 collective-permute-start.1
  83.9 0.1 pad_add_fusion.1.src_ref
  84.0 25.7 %collective-permute-done.1.sh = f32[8,64,128]{2,1,0:T(8,128)S(1)} collective-permute-done((f32[8,64,128]{2,1,0:T(8,128)S(1)}, f32[8,64,128]{2,1,0:T(8,128)S(1)}, u32[]{:S(2)}, u32[]{:S(2)}) %collective-permute-start.1) | collective-permute-done | bytes 262176 | tf_op jit(solution)/shard_map/halo_speed/ppermute | solution.py:216
  109.7 14.9 %forward.1 = (f32[8,8,64,128]{3,2,1,0:T(8,128)S(1)}, f32[8,256]{1,0:T(8,128)S(1)}) custom-call(s32[3]{0:T(128)S(1)} %pad_add_fusion.1.src_ref, f32[8]{0:T(128)S(1)} %bitcast.53, s32[2,256]{1,0:T(2,128)S(1)} %pad_add_fusion.rec_ref, f32[8,256]{1,0:T(8,128)S(1)} %bitcast.52, f32[8,64,128]{2,1,0:T(8,128)S(1)} %collective-permute-done.sl, ...), custom_call_target="tpu_custom_call" | custom-call | tf_op jit(solution)/shard_map/forward/pallas_call | solution.py:256
  124.7 6.8 %collective-permute-start.6 = (f32[8,256]{1,0:T(8,128)S(1)}, f32[8,256]{1,0:T(8,128)S(1)}, u32[]{:S(2)}, u32[]{:S(2)}) collective-permute-start(f32[8,256]{1,0:T(8,128)S(1)} %get-tuple-element.7.ro), channel_id=1, source_target_pairs={{0,1},{1,2},{2,3},{3,4},{4,5},{5,6},{6,7},{7,8},{8,9},{9,10},{10,1... | collective-permute-start | bytes 24584 | tf_op jit(solution)/shard_map/residuals/ppermute | solution.py:216
  131.4 0.0 collective-permute-done.10.cl
  131.5 1.5 collective-permute-start.7
  132.9 0.0 collective-permute-done.11.ch
  132.9 0.0 collective-permute-done.8.pl_
  133.0 0.0 collective-permute-done.9.ph
  133.0 0.0 collective-permute-done.6.rl
  133.0 3.8 %collective-permute-done.7.rh = f32[8,256]{1,0:T(8,128)S(1)} collective-permute-done((f32[8,256]{1,0:T(8,128)S(1)}, f32[8,256]{1,0:T(8,128)S(1)}, u32[]{:S(2)}, u32[]{:S(2)}) %collective-permute-start.7) | collective-permute-done | bytes 8224 | tf_op jit(solution)/shard_map/residuals/ppermute | solution.py:216
  136.7 19.9 %adjoint.1 = f32[8,64,128]{2,1,0:T(8,128)S(1)} custom-call(s32[2,256]{1,0:T(2,128)S(1)} %pad_add_fusion.rec_ref, f32[8,256]{1,0:T(8,128)S(1)} %collective-permute-done.6.rl, f32[8,256]{1,0:T(8,128)S(1)} %get-tuple-element.7.ro, f32[8,256]{1,0:T(8,128)S(1)} %collective-permute-done.7.rh, f32[8,64,128]{2,1,0:T(8,128)S(1)} %collective-permute-done.sl, ...), custom_call_target="tpu_custom_call" | custom-call | tf_op jit(solution)/shard_map/adjoint/pallas_call | solution.py:270
  156.6 31.2 %all_to_all.20 = f32[256,2,128]{2,1,0:T(2,128)S(1)} all-to-all(f32[256,2,128]{2,1,0:T(2,128)S(1)} %bitcast.38), channel_id=1, replica_groups=mesh['shot'=16,'sub'=16] {'shot','sub'}, dimensions={0} | all-to-all | bytes 524288 | tf_op jit(solution)/shard_map/spread_gradient/all_to_all | solution.py:280
  187.9 1.0 drop_gradient.1
  188.9 26.1 %all_to_all.21 = f32[256,4,128]{2,1,0:T(4,128)S(1)} all-to-all(f32[256,4,128]{2,1,0:T(4,128)S(1)} %bitcast.37), channel_id=1, replica_groups=mesh['shot'=16,'sub'=16] {'shot','sub'}, dimensions={0} | all-to-all | bytes 1048576 | tf_op jit(solution)/shard_map/deliver_gradient/all_to_all | solution.py:290
  215.0 1.0 copy.17
  (16 shorter events, 0.1 us)
Async XLA Ops:
  0.0 17.8 %copy-start.8 = (s32[16,2]{0,1:T(2,128)S(1)}, s32[16,2]{0,1:T(2,128)}, u32[]{:S(2)}) copy-start(s32[16,2]{0,1:T(2,128)} %param.13) | copy-start | bytes 388
  0.0 18.0 %copy-start.6 = (s32[512]{0:T(512)S(1)}, s32[512]{0:T(512)}, u32[]{:S(2)}) copy-start(s32[512]{0:T(512)} %param.12) | copy-start | bytes 6148
  0.0 45.7 %copy-start = (f32[1,8,64,128]{3,2,1,0:T(8,128)S(1)}, f32[1,8,64,128]{3,2,1,0:T(8,128)}, u32[]{:S(2)}) copy-start(f32[1,8,64,128]{3,2,1,0:T(8,128)} %param.18) | copy-start | bytes 786436
  0.0 51.4 %copy-start.1 = (f32[1,8,64,128]{3,2,1,0:T(8,128)S(1)}, f32[1,8,64,128]{3,2,1,0:T(8,128)}, u32[]{:S(2)}) copy-start(f32[1,8,64,128]{3,2,1,0:T(8,128)} %param.19) | copy-start | bytes 786436
  0.0 65.2 %copy-start.3 = (f32[1,8,64,128]{3,2,1,0:T(8,128)S(1)}, f32[1,8,64,128]{3,2,1,0:T(8,128)}, u32[]{:S(2)}) copy-start(f32[1,8,64,128]{3,2,1,0:T(8,128)} %param.21) | copy-start | bytes 786436
  0.0 75.0 %copy-start.2 = (f32[1,8,64,128]{3,2,1,0:T(8,128)S(1)}, f32[1,8,64,128]{3,2,1,0:T(8,128)}, u32[]{:S(2)}) copy-start(f32[1,8,64,128]{3,2,1,0:T(8,128)} %param.20) | copy-start | bytes 786436
  0.0 83.2 %copy-start.7 = (s32[1,256]{1,0:T(1,128)S(1)}, s32[1,256]{1,0:T(1,128)}, u32[]{:S(2)}) copy-start(s32[1,256]{1,0:T(1,128)} %param.16) | copy-start | bytes 3076
  0.0 109.7 %copy-start.5 = (f32[1,8]{1,0:T(1,128)S(1)}, f32[1,8]{1,0:T(1,128)}, u32[]{:S(2)}) copy-start(f32[1,8]{1,0:T(1,128)} %param.15) | copy-start | bytes 100
  0.1 109.7 %copy-start.4 = (f32[1,8,256]{2,1,0:T(8,128)S(1)}, f32[1,8,256]{2,1,0:T(8,128)}, u32[]{:S(2)}) copy-start(f32[1,8,256]{2,1,0:T(8,128)} %param.17) | copy-start | bytes 24580
  2.2 36.6 %all-to-all-start = ((f32[256,4,128]{2,1,0:T(4,128)}), f32[256,4,128]{2,1,0:T(4,128)S(1)}, u32[]{:S(2)}, u32[]{:S(2)}) async-start(f32[256,4,128]{2,1,0:T(4,128)} %bitcast.10), calls=%async_computation | async-start | bytes 1048576 | tf_op jit(solution)/shard_map/spread_velocity/all_to_all | solution.py:230
  40.5 20.5 %all-to-all-start.1 = ((f32[256,2,128]{2,1,0:T(2,128)}), f32[256,2,128]{2,1,0:T(2,128)S(1)}, u32[]{:S(2)}, u32[]{:S(2)}) async-start(f32[256,2,128]{2,1,0:T(2,128)} %bitcast.12), calls=%async_computation.1 | async-start | bytes 524288 | tf_op jit(solution)/shard_map/deliver_velocity/all_to_all | solution.py:240
  45.7 19.5 %collective-permute-start.2 = (f32[8,64,128]{2,1,0:T(8,128)S(1)}, f32[8,64,128]{2,1,0:T(8,128)S(1)}, u32[]{:S(2)}, u32[]{:S(2)}) collective-permute-start(f32[8,64,128]{2,1,0:T(8,128)S(1)} %bitcast.40), channel_id=1, source_target_pairs={{0,1},{1,2},{2,3},{3,4},{4,5},{5,6},{6,7},{7,8},{8,9},{9,10},{10,1... | collective-permute-start | bytes 786440 | tf_op jit(solution)/shard_map/halo_fwd/ppermute | solution.py:216
  50.1 23.6 %collective-permute-start.3 = (f32[8,64,128]{2,1,0:T(8,128)S(1)}, f32[8,64,128]{2,1,0:T(8,128)S(1)}, u32[]{:S(2)}, u32[]{:S(2)}) collective-permute-start(f32[8,64,128]{2,1,0:T(8,128)S(1)} %bitcast.41), channel_id=1, source_target_pairs={{1,0},{2,1},{3,2},{4,3},{5,4},{6,5},{7,6},{8,7},{9,8},{10,9},{11,1... | collective-permute-start | bytes 786440 | tf_op jit(solution)/shard_map/halo_fwd/ppermute | solution.py:216
  51.4 23.6 %collective-permute-start.4 = (f32[8,64,128]{2,1,0:T(8,128)S(1)}, f32[8,64,128]{2,1,0:T(8,128)S(1)}, u32[]{:S(2)}, u32[]{:S(2)}) collective-permute-start(f32[8,64,128]{2,1,0:T(8,128)S(1)} %bitcast.43), channel_id=1, source_target_pairs={{0,1},{1,2},{2,3},{3,4},{4,5},{5,6},{6,7},{7,8},{8,9},{9,10},{10,1... | collective-permute-start | bytes 786440 | tf_op jit(solution)/shard_map/halo_fwd/ppermute | solution.py:216
  57.8 22.8 %collective-permute-start.5 = (f32[8,64,128]{2,1,0:T(8,128)S(1)}, f32[8,64,128]{2,1,0:T(8,128)S(1)}, u32[]{:S(2)}, u32[]{:S(2)}) collective-permute-start(f32[8,64,128]{2,1,0:T(8,128)S(1)} %bitcast.44), channel_id=1, source_target_pairs={{1,0},{2,1},{3,2},{4,3},{5,4},{6,5},{7,6},{8,7},{9,8},{10,9},{11,1... | collective-permute-start | bytes 786440 | tf_op jit(solution)/shard_map/halo_fwd/ppermute | solution.py:216
  61.1 20.9 %collective-permute-start = (f32[8,64,128]{2,1,0:T(8,128)S(1)}, f32[8,64,128]{2,1,0:T(8,128)S(1)}, u32[]{:S(2)}, u32[]{:S(2)}) collective-permute-start(f32[8,64,128]{2,1,0:T(8,128)S(1)} %bitcast.32), channel_id=1, source_target_pairs={{0,1},{1,2},{2,3},{3,4},{4,5},{5,6},{6,7},{7,8},{8,9},{9,10},{10,1... | collective-permute-start | bytes 786440 | tf_op jit(solution)/shard_map/halo_speed/ppermute | solution.py:216
  65.2 66.2 %collective-permute-start.10 = (f32[8,64,128]{2,1,0:T(8,128)S(1)}, f32[8,64,128]{2,1,0:T(8,128)S(1)}, u32[]{:S(2)}, u32[]{:S(2)}) collective-permute-start(f32[8,64,128]{2,1,0:T(8,128)S(1)} %bitcast.49), channel_id=1, source_target_pairs={{0,1},{1,2},{2,3},{3,4},{4,5},{5,6},{6,7},{7,8},{8,9},{9,10},{10,1... | collective-permute-start | bytes 786440 | tf_op jit(solution)/shard_map/halo_adj/ppermute | solution.py:216
  73.7 59.2 %collective-permute-start.11 = (f32[8,64,128]{2,1,0:T(8,128)S(1)}, f32[8,64,128]{2,1,0:T(8,128)S(1)}, u32[]{:S(2)}, u32[]{:S(2)}) collective-permute-start(f32[8,64,128]{2,1,0:T(8,128)S(1)} %bitcast.50), channel_id=1, source_target_pairs={{1,0},{2,1},{3,2},{4,3},{5,4},{6,5},{7,6},{8,7},{9,8},{10,9},{11,1... | collective-permute-start | bytes 786440 | tf_op jit(solution)/shard_map/halo_adj/ppermute | solution.py:216
  75.0 57.9 %collective-permute-start.8 = (f32[8,64,128]{2,1,0:T(8,128)S(1)}, f32[8,64,128]{2,1,0:T(8,128)}, u32[]{:S(2)}, u32[]{:S(2)}) collective-permute-start(f32[8,64,128]{2,1,0:T(8,128)S(1)} %bitcast.46), channel_id=1, source_target_pairs={{0,1},{1,2},{2,3},{3,4},{4,5},{5,6},{6,7},{7,8},{8,9},{9,10},{10,1... | collective-permute-start | bytes 786440 | tf_op jit(solution)/shard_map/halo_adj/ppermute | solution.py:216
  80.6 52.3 %collective-permute-start.9 = (f32[8,64,128]{2,1,0:T(8,128)S(1)}, f32[8,64,128]{2,1,0:T(8,128)}, u32[]{:S(2)}, u32[]{:S(2)}) collective-permute-start(f32[8,64,128]{2,1,0:T(8,128)S(1)} %bitcast.47), channel_id=1, source_target_pairs={{1,0},{2,1},{3,2},{4,3},{5,4},{6,5},{7,6},{8,7},{9,8},{10,9},{11,1... | collective-permute-start | bytes 786440 | tf_op jit(solution)/shard_map/halo_adj/ppermute | solution.py:216
  81.9 27.8 %collective-permute-start.1 = (f32[8,64,128]{2,1,0:T(8,128)S(1)}, f32[8,64,128]{2,1,0:T(8,128)S(1)}, u32[]{:S(2)}, u32[]{:S(2)}) collective-permute-start(f32[8,64,128]{2,1,0:T(8,128)S(1)} %bitcast.33), channel_id=1, source_target_pairs={{1,0},{2,1},{3,2},{4,3},{5,4},{6,5},{7,6},{8,7},{9,8},{10,9},{11,1... | collective-permute-start | bytes 786440 | tf_op jit(solution)/shard_map/halo_speed/ppermute | solution.py:216
  124.7 8.3 %collective-permute-start.6 = (f32[8,256]{1,0:T(8,128)S(1)}, f32[8,256]{1,0:T(8,128)S(1)}, u32[]{:S(2)}, u32[]{:S(2)}) collective-permute-start(f32[8,256]{1,0:T(8,128)S(1)} %get-tuple-element.7.ro), channel_id=1, source_target_pairs={{0,1},{1,2},{2,3},{3,4},{4,5},{5,6},{6,7},{7,8},{8,9},{9,10},{10,1... | collective-permute-start | bytes 24584 | tf_op jit(solution)/shard_map/residuals/ppermute | solution.py:216
  131.5 5.3 %collective-permute-start.7 = (f32[8,256]{1,0:T(8,128)S(1)}, f32[8,256]{1,0:T(8,128)S(1)}, u32[]{:S(2)}, u32[]{:S(2)}) collective-permute-start(f32[8,256]{1,0:T(8,128)S(1)} %get-tuple-element.7.ro), channel_id=1, source_target_pairs={{1,0},{2,1},{3,2},{4,3},{5,4},{6,5},{7,6},{8,7},{9,8},{10,9},{11,1... | collective-permute-start | bytes 24584 | tf_op jit(solution)/shard_map/residuals/ppermute | solution.py:216

commit v2 on v1

--- a/solution.py
+++ b/solution.py
@@ -43,10 +43,30 @@
     out_ref[...] = dot3(onehot, x_ref[...], ((1,), (0,)))
 
 
-def load_field(dst, low, own, high):
+def each(lo, hi, body):
+    for x in range(lo, hi):
+        body(x, 0)
+
+
+def tile_half(speed3, block, half, ny):
+    n = T * ny // 2
+    value = speed3[pl.ds(2 * block + half, n, stride=6), :]
+    return value.reshape(T // 2, ny, LANES)
+
+
+def square_speed(dst, speed3, ny):
+    for block in range(3):
+        for half in range(2):
+            value = tile_half(speed3, block, half, ny)
+            first = block * T + half * (T // 2)
+            dst[first : first + T // 2] = value * value
+
+
+def load_field(dst, edge_ref, low, own, high):
     ny = own.shape[1]
-    for block, ref in enumerate((low, own, high)):
-        dst[block * T : (block + 1) * T, PADY : PADY + ny, :] = ref[...]
+    dst[0:T, PADY : PADY + ny, :] = jnp.where(edge_ref[0] > 0, low[...], 0.0)
+    dst[T : 2 * T, PADY : PADY + ny, :] = own[...]
+    dst[2 * T : 3 * T, PADY : PADY + ny, :] = jnp.where(edge_ref[1] > 0, high[...], 0.0)
 
 
 def clear_pad(dst, ny):
@@ -66,19 +86,17 @@
 
 
 def forward_kernel(
-    src_ref, wave_ref, rec_ref, obs_ref,
-    sl, so, sh, pl_, po, ph, cl, co, ch,
+    edge_ref, src_ref, wave_ref, rec_ref, obs_ref,
+    speed3, low, po, co, high,
     lap_ref, res_ref, prev, cur, speed_sq,
 ):
-    ny = so.shape[1]
+    ny = po.shape[1]
     rows = T * ny
     clear_pad(prev, ny)
     clear_pad(cur, ny)
-    load_field(prev, pl_, po, ph)
-    load_field(cur, cl, co, ch)
-    for block, ref in enumerate((sl, so, sh)):
-        value = ref[...]
-        speed_sq[block * T : (block + 1) * T] = value * value
+    load_field(prev, edge_ref, low.at[0], po, high.at[0])
+    load_field(cur, edge_ref, low.at[1], co, high.at[1])
+    square_speed(speed_sq, speed3, ny)
     lane = lax.broadcasted_iota(jnp.int32, (ny, LANES), 1)
     first, last = lane == 0, lane == LANES - 1
     src_x, src_y, src_z = src_ref[0], src_ref[1], src_ref[2]
@@ -104,9 +122,9 @@
             lap_ref[n, x - T] = update(x, True)
             return carry
 
-        lax.fori_loop(1 + n, T, outer, 0)
-        lax.fori_loop(T, 2 * T, inner, 0)
-        lax.fori_loop(2 * T, 3 * T - 1 - n, outer, 0)
+        each(1 + n, T, outer)
+        each(T, 2 * T, inner)
+        each(2 * T, 3 * T - 1 - n, outer)
 
         @pl.when(inside)
         def _():
@@ -123,20 +141,20 @@
 
 
 def adjoint_kernel(
-    rec_ref, rl, ro, rh,
-    sl, so, sh, pl_, po, ph, cl, co, ch, lap_ref,
-    out_ref, prev, cur, speed_sq, inject,
+    edge_ref, rec_ref, rl, ro, rh,
+    speed3, low, po, co, high, lap_ref,
+    out_ref, prev, cur, speed_sq, inject, speed,
 ):
-    ny = so.shape[1]
+    ny = po.shape[1]
     clear_pad(prev, ny)
     clear_pad(cur, ny)
-    load_field(prev, pl_, po, ph)
-    load_field(cur, cl, co, ch)
-    for block, ref in enumerate((sl, so, sh)):
-        value = ref[...]
-        speed_sq[block * T : (block + 1) * T] = value * value
+    load_field(prev, edge_ref, low.at[0], po, high.at[0])
+    load_field(cur, edge_ref, low.at[1], co, high.at[1])
+    square_speed(speed_sq, speed3, ny)
     lane = lax.broadcasted_iota(jnp.int32, (ny, LANES), 1)
     first, last = lane == 0, lane == LANES - 1
+    for half in range(2):
+        speed[half * (T // 2) : (half + 1) * (T // 2)] = tile_half(speed3, 1, half, ny)
     rec = rec_ref[...]
     resid = rl[...] + ro[...] + rh[...]
     z_mask = lax.broadcasted_iota(jnp.int32, (LANES, REC), 0) == rec[1:2]
@@ -163,7 +181,7 @@
 
         def inner(x, carry):
             new = update(x)
-            term = so[x - T] * new * lap_ref[n, x - T]
+            term = speed[x - T] * new * lap_ref[n, x - T]
             if k == 0:
                 out_ref[x - T] = term
             elif k == STEPS - 1:
@@ -172,9 +190,9 @@
                 out_ref[x - T] = out_ref[x - T] + term
             return carry
 
-        lax.fori_loop(lo, T, outer, 0)
-        lax.fori_loop(T, 2 * T, inner, 0)
-        lax.fori_loop(2 * T, hi, outer, 0)
+        each(lo, T, outer)
+        each(T, 2 * T, inner)
+        each(2 * T, hi, outer)
 
 
 def vmem():
@@ -187,6 +205,84 @@
 
 def params():
     return pltpu.CompilerParams(vmem_limit_bytes=48 * 1024 * 1024)
+
+
+def call_pick(index, x):
+    return pl.pallas_call(
+        pick_kernel,
+        out_shape=jax.ShapeDtypeStruct((index.shape[1], x.shape[1]), jnp.float32),
+        in_specs=[vmem(), vmem()],
+        out_specs=vmem(),
+        compiler_params=params(),
+    )(index, x)
+
+
+def cut_kernel(x_ref, out_ref):
+    k, n, _ = x_ref.shape
+    for i in range(k):
+        out_ref[pl.ds(i, n, stride=k), :] = x_ref[i]
+
+
+def call_cut(x):
+    return pl.pallas_call(
+        cut_kernel,
+        out_shape=jax.ShapeDtypeStruct((x.shape[0] * x.shape[1], x.shape[2]), jnp.float32),
+        in_specs=[vmem()],
+        out_specs=vmem(),
+        compiler_params=params(),
+    )(x)
+
+
+def stack_kernel(*refs):
+    fields, out, sems = refs[:-2], refs[-2], refs[-1]
+    copies = [pltpu.make_async_copy(f, out.at[i], sems.at[i]) for i, f in enumerate(fields)]
+    for c in copies:
+        c.start()
+    for c in copies:
+        c.wait()
+
+
+def call_stack(*fields):
+    anywhere = pl.BlockSpec(memory_space=pl.ANY)
+    return pl.pallas_call(
+        stack_kernel,
+        out_shape=jax.ShapeDtypeStruct((len(fields),) + fields[0].shape, jnp.float32),
+        in_specs=[anywhere] * len(fields),
+        out_specs=anywhere,
+        scratch_shapes=[pltpu.SemaphoreType.DMA((len(fields),))],
+        compiler_params=params(),
+    )(*fields)
+
+
+def call_forward(edge, src_place, wave, rec, obs, speed3, fields):
+    layers, ny, nz = fields[1].shape
+    field = pltpu.VMEM((3 * T, ny + 2 * PADY, nz), jnp.float32)
+    flat = pltpu.VMEM((3 * T, ny, nz), jnp.float32)
+    return pl.pallas_call(
+        forward_kernel,
+        out_shape=(
+            jax.ShapeDtypeStruct((STEPS, layers, ny, nz), jnp.float32),
+            jax.ShapeDtypeStruct((STEPS, REC), jnp.float32),
+        ),
+        in_specs=[smem()] * 3 + [vmem()] * 7,
+        out_specs=(vmem(), vmem()),
+        scratch_shapes=[field, field, flat],
+        compiler_params=params(),
+    )(edge, src_place, wave, rec, obs, speed3, *fields)
+
+
+def call_adjoint(edge, rec, res3, speed3, fields, laps):
+    layers, ny, nz = fields[1].shape
+    field = pltpu.VMEM((3 * T, ny + 2 * PADY, nz), jnp.float32)
+    flat = pltpu.VMEM((3 * T, ny, nz), jnp.float32)
+    return pl.pallas_call(
+        adjoint_kernel,
+        out_shape=jax.ShapeDtypeStruct((layers, ny, nz), jnp.float32),
+        in_specs=[smem()] + [vmem()] * 10,
+        out_specs=vmem(),
+        scratch_shapes=[field, field, flat, flat, pltpu.VMEM((T, ny, nz), jnp.float32)],
+        compiler_params=params(),
+    )(edge, rec, *res3, speed3, *fields, laps)
 
 
 def shards(
@@ -209,7 +305,7 @@
     local_slots, layers, ny, nz = velocity.shape
     rows = layers * ny
     piece = rows // n_all
-    forward = [(i, i + 1) for i in range(n_sub - 1)]
+    forward = [(i, (i + 1) % n_sub) for i in range(n_sub)]
     backward = [(j, i) for i, j in forward]
 
     def both(x):
@@ -220,61 +316,40 @@
     wanted = jnp.sum(jnp.where(table[:, None] == tiles[None, :], tile_slot[:, None], 0), axis=0)
     want_rows = (wanted[:, None] * piece + jnp.arange(piece, dtype=jnp.int32)).reshape(1, n_all * piece)
 
+    pad = jnp.pad(wanted.reshape(n_shot, n_sub), ((0, 0), (1, 1)), constant_values=-1)
+    near = jnp.stack([pad[:, :-2], pad[:, 1:-1], pad[:, 2:]], axis=-1)
+    wide_rows = jnp.where(
+        near[..., None] >= 0, near[..., None] * piece + jnp.arange(piece, dtype=jnp.int32), -1
+    ).reshape(1, n_all * 3 * piece)
+    edge = jnp.stack([sub_index > 0, sub_index < n_sub - 1]).astype(jnp.int32)
+
     cells = receiver_cells[0]
     rec = jnp.stack([cells // nz - sub_index * rows, cells % nz])
     src = source_cell[0]
     src_place = jnp.stack([src // (ny * nz) - (sub_index - 1) * layers, src // nz % ny, src % nz])
 
+    with jax.named_scope("halo_fields"):
+        low, high = both(call_stack(fwd_prev[0], fwd_curr[0]))
+        adj_low, adj_high = both(call_stack(adj_prev[0], adj_curr[0]))
     with jax.named_scope("spread_velocity"):
-        cut = velocity.reshape(local_slots, n_all, piece, nz).transpose(1, 0, 2, 3)
-        spread = lax.all_to_all(cut.reshape(n_all, local_slots * piece, nz), ALL, 0, 0, tiled=True)
+        cut = call_cut(velocity.reshape(local_slots * piece, n_all, nz))
+        spread = lax.all_to_all(cut.reshape(n_all, local_slots, piece, nz), ALL, 0, 0, tiled=True)
     with jax.named_scope("pick_velocity"):
-        picked = pl.pallas_call(
-            pick_kernel,
-            out_shape=jax.ShapeDtypeStruct((n_all * piece, nz), jnp.float32),
-            in_specs=[vmem(), vmem()],
-            out_specs=vmem(),
-            compiler_params=params(),
-        )(want_rows, spread.reshape(n_all * local_slots * piece, nz))
+        picked = call_pick(wide_rows, spread.reshape(n_all * local_slots * piece, nz))
+        picked, low, high = lax.optimization_barrier((picked, low, high))
     with jax.named_scope("deliver_velocity"):
-        speed = lax.all_to_all(picked.reshape(n_all, piece, nz), ALL, 0, 0, tiled=True).reshape(layers, ny, nz)
-
-    def triple(x):
-        low, high = both(x)
-        return low, x, high
-
-    with jax.named_scope("halo_fwd"):
-        prev3, cur3 = triple(fwd_prev[0]), triple(fwd_curr[0])
-    with jax.named_scope("halo_adj"):
-        aprev3, acur3 = triple(adj_prev[0]), triple(adj_curr[0])
-    with jax.named_scope("halo_speed"):
-        speed3 = triple(speed)
-
-    field = pltpu.VMEM((3 * T, ny + 2 * PADY, nz), jnp.float32)
-    flat = pltpu.VMEM((3 * T, ny, nz), jnp.float32)
+        speed3 = lax.all_to_all(picked.reshape(n_all, 3, piece, nz), ALL, 0, 0, tiled=True)
+        speed3 = speed3.reshape(n_all * 3 * piece, nz)
+
+    fwd4 = (low, fwd_prev[0], fwd_curr[0], high)
+    adj4 = (adj_low, adj_prev[0], adj_curr[0], adj_high)
     with jax.named_scope("forward"):
-        laps, resid = pl.pallas_call(
-            forward_kernel,
-            out_shape=(
-                jax.ShapeDtypeStruct((STEPS, layers, ny, nz), jnp.float32),
-                jax.ShapeDtypeStruct((STEPS, REC), jnp.float32),
-            ),
-            in_specs=[smem(), smem()] + [vmem()] * 11,
-            out_specs=(vmem(), vmem()),
-            scratch_shapes=[field, field, flat],
-            compiler_params=params(),
-        )(src_place, wavelet[0], rec, observed[0], *speed3, *prev3, *cur3)
+        laps, resid = call_forward(edge, src_place, wavelet[0], rec, observed[0], speed3, fwd4)
     with jax.named_scope("residuals"):
-        res3 = triple(resid)
+        res_low, res_high = both(resid)
+        res3 = (res_low, resid, res_high)
     with jax.named_scope("adjoint"):
-        image = pl.pallas_call(
-            adjoint_kernel,
-            out_shape=jax.ShapeDtypeStruct((layers, ny, nz), jnp.float32),
-            in_specs=[vmem()] * 14,
-            out_specs=vmem(),
-            scratch_shapes=[field, field, flat, flat],
-            compiler_params=params(),
-        )(rec, *res3, *speed3, *aprev3, *acur3, laps)
+        image = call_adjoint(edge, rec, res3, speed3, adj4, laps)
 
     with jax.named_scope("spread_gradient"):
         pieces = lax.all_to_all(image.reshape(n_all, piece, nz), ALL, 0, 0, tiled=True)

time: 217 us -> 165 us (0.76)
  blocking collectives: 57.3 us -> 26.1 us
  Pallas kernels: 37.6 us -> 15.9 us
  starting transfers between devices: 61.5 us -> 54 us
  waiting for transfers between devices: 54.7 us -> 59.3 us
  local copies, waits for them, and re-layouts: 3.33 us -> 7.24 us
    all_to_all x2 -> x3, waiting for transfers between devices: 22.3 us -> 56.8 us  [the longest x1 23.8 us: shards(): lax.all_to_all(cut.reshape(n_all, local_slots, piece, nz), ALL, 0, 0, til...]
    all_to_all x1 -> x0, blocking collectives: 31.2 us -> none  [shards(): lax.all_to_all(image.reshape(n_all, piece, nz), ALL, 0, 0, tiled=True)]
    ppermute x12 -> x6, waiting for transfers between devices: 32.5 us -> 2.5 us  [both(): return (lax.ppermute(x, 'sub', forward), lax.ppermute(x, 'sub', backward))]
    pallas_call x3 -> x6, Pallas kernels: 36.6 us -> 14.9 us  [the longest x1 5.52 us: call_adjoint(): pl.pallas_call(adjoint_kernel, out_shape=jax.ShapeDtypeStruct((layers, ny...]
    ppermute x12 -> x6, starting transfers between devices: 40.7 us -> 22.3 us  [both(): return (lax.ppermute(x, 'sub', forward), lax.ppermute(x, 'sub', backward))]
    all_to_all x2 -> x3, starting transfers between devices: 20.8 us -> 31.8 us  [the longest x1 12.1 us: shards(): lax.all_to_all(image.reshape(n_all, piece, nz), ALL, 0, 0, tiled=True)]
    unnamed x18 -> x32, local copies, waits for them, and re-layouts: 0.04 us -> 5.1 us
  transfers between devices with their start and end apart: 14 -> 9, of which waited for: 5 -> 5; matrix products, arithmetic and copies ran while one was open for 0% -> 1% of each run, Pallas kernels for 7% -> 6%
where the time goes in v2:
time: 165 us
  waiting for transfers between devices  59.3 us (36%)
  starting transfers between devices  54 us (33%)
  blocking collectives  26.1 us (16%)
  Pallas kernels  15.9 us (10%)
  local copies, waits for them, and re-layouts  7.24 us (4%)
    all_to_all x1, blocking collectives, shards(): lax.all_to_all(dropped.reshape(n_all, local_slots * piece, nz), ALL, 0, 0...  26.1 us
    all_to_all x1, waiting for transfers between devices, shards(): lax.all_to_all(cut.reshape(n_all, local_slots, piece, nz), ALL, 0, 0, til...  23.8 us
    ppermute x6, starting transfers between devices, both(): return (lax.ppermute(x, 'sub', forward), lax.ppermute(x, 'sub', backward))  22.3 us
    all_to_all x1, waiting for transfers between devices, shards(): lax.all_to_all(picked.reshape(n_all, 3, piece, nz), ALL, 0, 0, tiled=True)  17.9 us
    all_to_all x1, waiting for transfers between devices, shards(): lax.all_to_all(image.reshape(n_all, piece, nz), ALL, 0, 0, tiled=True)  15.1 us
    all_to_all x1, starting transfers between devices, shards(): lax.all_to_all(image.reshape(n_all, piece, nz), ALL, 0, 0, tiled=True)  12.1 us
    all_to_all x1, starting transfers between devices, shards(): lax.all_to_all(cut.reshape(n_all, local_slots, piece, nz), ALL, 0, 0, til...  10.7 us
    all_to_all x1, starting transfers between devices, shards(): lax.all_to_all(picked.reshape(n_all, 3, piece, nz), ALL, 0, 0, tiled=True)  9 us
  transfers between devices with their start and end apart: 9, of which 5 were waited for; matrix products, arithmetic and copies ran while one was open for 1% of the time, Pallas kernels for 6%

profile of v2, /device:TPU:1, one launch (start us, length us, event | category | flops | bytes accessed | tf_op | source)
XLA Modules:
  0.0 164.8 jit_solution(6538613370557094979)
XLA Ops:
  0.0 1.0 copy-done.2
  1.0 0.9 copy-done.4
  1.9 0.1 halo_fields.2
  2.0 3.9 %collective-permute-start = (f32[2,8,64,128]{3,2,1,0:T(8,128)S(1)}, f32[2,8,64,128]{3,2,1,0:T(8,128)S(1)}, u32[]{:S(2)}, u32[]{:S(2)}) collective-permute-start(f32[2,8,64,128]{3,2,1,0:T(8,128)S(1)} %halo_fields.2), channel_id=1, source_target_pairs={{0,1},{1,2},{2,3},{3,4},{4,5},{5,6},{6,7},{7,8},{8,9},{9,10},{10,1... | collective-permute-start | bytes 1572872 | tf_op jit(solution)/shard_map/halo_fields/ppermute | solution.py:312
  5.9 5.3 %collective-permute-start.1 = (f32[2,8,64,128]{3,2,1,0:T(8,128)S(1)}, f32[2,8,64,128]{3,2,1,0:T(8,128)S(1)}, u32[]{:S(2)}, u32[]{:S(2)}) collective-permute-start(f32[2,8,64,128]{3,2,1,0:T(8,128)S(1)} %halo_fields.2), channel_id=1, source_target_pairs={{1,0},{2,1},{3,2},{4,3},{5,4},{6,5},{7,6},{8,7},{9,8},{10,9},{11,1... | collective-permute-start | bytes 1572872 | tf_op jit(solution)/shard_map/halo_fields/ppermute | solution.py:312
  11.2 1.0 copy-done.6
  12.3 0.9 spread_velocity.1
  13.1 10.7 %all-to-all-start = ((f32[256,2,2,128]{3,2,1,0:T(2,128)}), f32[256,2,2,128]{3,2,1,0:T(2,128)S(1)}, u32[]{:S(2)}, u32[]{:S(2)}) async-start(f32[256,2,2,128]{3,2,1,0:T(2,128)} %bitcast.13), calls=%async_computation | async-start | bytes 1048576 | tf_op jit(solution)/shard_map/spread_velocity/all_to_all | solution.py:336
  23.8 0.1 multiply_add_fusion
  23.9 0.1 add.109
  24.0 0.2 select_reduce_fusion
  24.1 0.1 reshape.176
  24.2 0.1 stack.47
  24.3 0.1 slice_bitcast_fusion.1
  24.4 0.2 copy.18
  24.5 0.0 copy-start.1
  24.6 0.2 copy.17
  24.8 0.7 add_select_fusion
  25.5 0.3 select_n.57.index_ref
  25.8 0.0 copy-start.14
  25.8 0.0 copy-start.3
  25.8 0.0 copy-start.5
  25.9 0.0 copy-start.11
  25.9 0.0 copy-start.12
  25.9 23.8 %all-to-all-done = f32[256,2,2,128]{3,2,1,0:T(2,128)S(1)} async-done(((f32[256,2,2,128]{3,2,1,0:T(2,128)}), f32[256,2,2,128]{3,2,1,0:T(2,128)S(1)}, u32[]{:S(2)}, u32[]{:S(2)}) %all-to-all-start) | async-done | bytes 524320 | tf_op jit(solution)/shard_map/spread_velocity/all_to_all | solution.py:336
  49.7 3.6 %pick_velocity.1 = f32[1536,128]{1,0:T(8,128)} custom-call(s32[1,1536]{1,0:T(1,128)S(1)} %select_n.57.index_ref, f32[1024,128]{1,0:T(8,128)S(1)} %bitcast.38), custom_call_target="tpu_custom_call" | custom-call | tf_op jit(solution)/shard_map/pick_velocity/pallas_call | solution.py:211
  53.3 9.0 %all-to-all-start.1 = ((f32[256,3,2,128]{3,2,1,0:T(2,128)}), f32[256,3,2,128]{3,2,1,0:T(2,128)S(1)}, u32[]{:S(2)}, u32[]{:S(2)}) async-start(f32[256,3,2,128]{3,2,1,0:T(2,128)} %bitcast.17), calls=%async_computation.1 | async-start | bytes 1572864 | tf_op jit(solution)/shard_map/deliver_velocity/all_to_all | solution.py:341
  62.3 0.1 halo_fields.3
  62.4 2.8 %collective-permute-start.4 = (f32[2,8,64,128]{3,2,1,0:T(8,128)S(1)}, f32[2,8,64,128]{3,2,1,0:T(8,128)S(1)}, u32[]{:S(2)}, u32[]{:S(2)}) collective-permute-start(f32[2,8,64,128]{3,2,1,0:T(8,128)S(1)} %halo_fields.3), channel_id=1, source_target_pairs={{0,1},{1,2},{2,3},{3,4},{4,5},{5,6},{6,7},{7,8},{8,9},{9,10},{10,1... | collective-permute-start | bytes 1572872 | tf_op jit(solution)/shard_map/halo_fields/ppermute | solution.py:312
  65.2 4.5 %collective-permute-start.5 = (f32[2,8,64,128]{3,2,1,0:T(8,128)S(1)}, f32[2,8,64,128]{3,2,1,0:T(8,128)S(1)}, u32[]{:S(2)}, u32[]{:S(2)}) collective-permute-start(f32[2,8,64,128]{3,2,1,0:T(8,128)S(1)} %halo_fields.3), channel_id=1, source_target_pairs={{1,0},{2,1},{3,2},{4,3},{5,4},{6,5},{7,6},{8,7},{9,8},{10,9},{11,1... | collective-permute-start | bytes 1572872 | tf_op jit(solution)/shard_map/halo_fields/ppermute | solution.py:312
  70.4 0.1 add_convert_fusion.edge_ref
  70.5 0.1 pad_add_fusion.2.src_ref
  70.6 17.9 %all-to-all-done.1 = f32[256,3,2,128]{3,2,1,0:T(2,128)S(1)} async-done(((f32[256,3,2,128]{3,2,1,0:T(2,128)}), f32[256,3,2,128]{3,2,1,0:T(2,128)S(1)}, u32[]{:S(2)}, u32[]{:S(2)}) %all-to-all-start.1) | async-done | bytes 786464 | tf_op jit(solution)/shard_map/deliver_velocity/all_to_all | solution.py:341
  88.6 1.0 copy-done.8
  89.6 1.0 copy-done.10
  90.6 4.8 %forward.1 = (f32[8,8,64,128]{3,2,1,0:T(8,128)S(1)}, f32[8,256]{1,0:T(8,128)S(1)}) custom-call(s32[2]{0:T(128)S(1)} %add_convert_fusion.edge_ref, s32[3]{0:T(128)S(1)} %pad_add_fusion.2.src_ref, f32[8]{0:T(128)S(1)} %bitcast.51, s32[2,256]{1,0:T(2,128)S(1)} %pad_add_fusion.1.rec_ref, f32[8,256]{1,0:T(8,128)S(1)} %bitcast.50, f32[1536,128]{1,0:T(8,128)S(1)} %bitcast.36, ...), custom_call_target="tpu_custom_call" | custom-call | tf_op jit(solution)/shard_map/forward/pallas_call | solution.py:261
  95.5 1.7 %collective-permute-start.2 = (f32[8,256]{1,0:T(8,128)S(1)}, f32[8,256]{1,0:T(8,128)S(1)}, u32[]{:S(2)}, u32[]{:S(2)}) collective-permute-start(f32[8,256]{1,0:T(8,128)S(1)} %get-tuple-element.13.ro), channel_id=1, source_target_pairs={{0,1},{1,2},{2,3},{3,4},{4,5},{5,6},{6,7},{7,8},{8,9},{9,10},{10,1... | collective-permute-start | bytes 24584 | tf_op jit(solution)/shard_map/residuals/ppermute | solution.py:312
  97.2 4.1 %collective-permute-start.3 = (f32[8,256]{1,0:T(8,128)S(1)}, f32[8,256]{1,0:T(8,128)S(1)}, u32[]{:S(2)}, u32[]{:S(2)}) collective-permute-start(f32[8,256]{1,0:T(8,128)S(1)} %get-tuple-element.13.ro), channel_id=1, source_target_pairs={{1,0},{2,1},{3,2},{4,3},{5,4},{6,5},{7,6},{8,7},{9,8},{10,9},{11,1... | collective-permute-start | bytes 24584 | tf_op jit(solution)/shard_map/residuals/ppermute | solution.py:312
  101.3 2.3 %collective-permute-done.5.high = f32[2,8,64,128]{3,2,1,0:T(8,128)S(1)} collective-permute-done((f32[2,8,64,128]{3,2,1,0:T(8,128)S(1)}, f32[2,8,64,128]{3,2,1,0:T(8,128)S(1)}, u32[]{:S(2)}, u32[]{:S(2)}) %collective-permute-start.5) | collective-permute-done | bytes 524320 | tf_op jit(solution)/shard_map/halo_fields/ppermute | solution.py:312
  103.6 0.2 collective-permute-done.3.rh
  103.8 5.5 %adjoint.1 = f32[8,64,128]{2,1,0:T(8,128)} custom-call(s32[2]{0:T(128)S(1)} %add_convert_fusion.edge_ref, s32[2,256]{1,0:T(2,128)S(1)} %pad_add_fusion.1.rec_ref, f32[8,256]{1,0:T(8,128)S(1)} %collective-permute-done.2.rl, f32[8,256]{1,0:T(8,128)S(1)} %get-tuple-element.13.ro, f32[8,256]{1,0:T(8,128)S(1)} %collective-permute-done.3.rh, ...), custom_call_target="tpu_custom_call" | custom-call | tf_op jit(solution)/shard_map/adjoint/pallas_call | solution.py:278
  109.3 12.1 %all-to-all-start.2 = ((f32[256,2,128]{2,1,0:T(2,128)}), f32[256,2,128]{2,1,0:T(2,128)S(1)}, u32[]{:S(2)}, u32[]{:S(2)}) async-start(f32[256,2,128]{2,1,0:T(2,128)} %bitcast.21), calls=%async_computation.2 | async-start | bytes 524288 | tf_op jit(solution)/shard_map/spread_gradient/all_to_all | solution.py:355
  121.4 0.1 iota_add_fusion
  121.5 0.1 add.113.index_ref
  121.6 15.1 %all-to-all-done.2 = f32[256,2,128]{2,1,0:T(2,128)S(1)} async-done(((f32[256,2,128]{2,1,0:T(2,128)}), f32[256,2,128]{2,1,0:T(2,128)S(1)}, u32[]{:S(2)}, u32[]{:S(2)}) %all-to-all-start.2) | async-done | bytes 262176 | tf_op jit(solution)/shard_map/spread_gradient/all_to_all | solution.py:355
  136.7 1.0 drop_gradient.1
  137.7 26.1 %all_to_all.20 = f32[256,4,128]{2,1,0:T(4,128)S(1)} all-to-all(f32[256,4,128]{2,1,0:T(4,128)S(1)} %bitcast.39), channel_id=1, replica_groups=mesh['shot'=16,'sub'=16] {'shot','sub'}, dimensions={0} | all-to-all | bytes 1048576 | tf_op jit(solution)/shard_map/deliver_gradient/all_to_all | solution.py:365
  163.8 1.0 copy.19
  (31 shorter events, 0.1 us)
Async XLA Ops:
  0.0 23.8 %copy-start.15 = (s32[16,2]{0,1:T(2,128)S(1)}, s32[16,2]{0,1:T(2,128)}, u32[]{:S(2)}) copy-start(s32[16,2]{0,1:T(2,128)} %param.13) | copy-start | bytes 388
  0.0 24.0 %copy-start.13 = (s32[512]{0:T(512)S(1)}, s32[512]{0:T(512)}, u32[]{:S(2)}) copy-start(s32[512]{0:T(512)} %param.12) | copy-start | bytes 6148
  0.0 1.0 copy-start.2
  1.0 0.9 copy-start.4
  2.0 51.3 %collective-permute-start = (f32[2,8,64,128]{3,2,1,0:T(8,128)S(1)}, f32[2,8,64,128]{3,2,1,0:T(8,128)S(1)}, u32[]{:S(2)}, u32[]{:S(2)}) collective-permute-start(f32[2,8,64,128]{3,2,1,0:T(8,128)S(1)} %halo_fields.2), channel_id=1, source_target_pairs={{0,1},{1,2},{2,3},{3,4},{4,5},{5,6},{6,7},{7,8},{8,9},{9,10},{10,1... | collective-permute-start | bytes 1572872 | tf_op jit(solution)/shard_map/halo_fields/ppermute | solution.py:312
  5.9 47.4 %collective-permute-start.1 = (f32[2,8,64,128]{3,2,1,0:T(8,128)S(1)}, f32[2,8,64,128]{3,2,1,0:T(8,128)S(1)}, u32[]{:S(2)}, u32[]{:S(2)}) collective-permute-start(f32[2,8,64,128]{3,2,1,0:T(8,128)S(1)} %halo_fields.2), channel_id=1, source_target_pairs={{1,0},{2,1},{3,2},{4,3},{5,4},{6,5},{7,6},{8,7},{9,8},{10,9},{11,1... | collective-permute-start | bytes 1572872 | tf_op jit(solution)/shard_map/halo_fields/ppermute | solution.py:312
  11.2 1.0 copy-start.6
  13.1 36.6 %all-to-all-start = ((f32[256,2,2,128]{3,2,1,0:T(2,128)}), f32[256,2,2,128]{3,2,1,0:T(2,128)S(1)}, u32[]{:S(2)}, u32[]{:S(2)}) async-start(f32[256,2,2,128]{3,2,1,0:T(2,128)} %bitcast.13), calls=%async_computation | async-start | bytes 1048576 | tf_op jit(solution)/shard_map/spread_velocity/all_to_all | solution.py:336
  24.5 37.8 %copy-start = (f32[1,8,64,128]{3,2,1,0:T(8,128)S(1)}, f32[1,8,64,128]{3,2,1,0:T(8,128)}, u32[]{:S(2)}) copy-start(f32[1,8,64,128]{3,2,1,0:T(8,128)} %param.20) | copy-start | bytes 786436
  24.5 37.8 %copy-start.1 = (f32[1,8,64,128]{3,2,1,0:T(8,128)S(1)}, f32[1,8,64,128]{3,2,1,0:T(8,128)}, u32[]{:S(2)}) copy-start(f32[1,8,64,128]{3,2,1,0:T(8,128)} %param.21) | copy-start | bytes 786436
  25.8 44.8 %copy-start.14 = (s32[1,256]{1,0:T(1,128)S(1)}, s32[1,256]{1,0:T(1,128)}, u32[]{:S(2)}) copy-start(s32[1,256]{1,0:T(1,128)} %param.16) | copy-start | bytes 3076
  25.8 62.7 %copy-start.3 = (f32[1,8,64,128]{3,2,1,0:T(8,128)S(1)}, f32[1,8,64,128]{3,2,1,0:T(8,128)}, u32[]{:S(2)}) copy-start(f32[1,8,64,128]{3,2,1,0:T(8,128)} %param.18) | copy-start | bytes 786436
  25.8 62.7 %copy-start.5 = (f32[1,8,64,128]{3,2,1,0:T(8,128)S(1)}, f32[1,8,64,128]{3,2,1,0:T(8,128)}, u32[]{:S(2)}) copy-start(f32[1,8,64,128]{3,2,1,0:T(8,128)} %param.19) | copy-start | bytes 786436
  25.9 62.7 %copy-start.11 = (f32[1,8,256]{2,1,0:T(8,128)S(1)}, f32[1,8,256]{2,1,0:T(8,128)}, u32[]{:S(2)}) copy-start(f32[1,8,256]{2,1,0:T(8,128)} %param.17) | copy-start | bytes 24580
  25.9 62.7 %copy-start.12 = (f32[1,8]{1,0:T(1,128)S(1)}, f32[1,8]{1,0:T(1,128)}, u32[]{:S(2)}) copy-start(f32[1,8]{1,0:T(1,128)} %param.15) | copy-start | bytes 100
  53.3 9.1 %copy-start.7 = (f32[2,8,64,128]{3,2,1,0:T(8,128)}, f32[2,8,64,128]{3,2,1,0:T(8,128)S(1)}, u32[]{:S(2)}) copy-start(f32[2,8,64,128]{3,2,1,0:T(8,128)S(1)} %collective-permute-done.low) | copy-start | bytes 1572868
  53.3 9.0 %copy-start.9 = (f32[2,8,64,128]{3,2,1,0:T(8,128)}, f32[2,8,64,128]{3,2,1,0:T(8,128)S(1)}, u32[]{:S(2)}) copy-start(f32[2,8,64,128]{3,2,1,0:T(8,128)S(1)} %collective-permute-done.1.high) | copy-start | bytes 1572868
  53.3 35.2 %all-to-all-start.1 = ((f32[256,3,2,128]{3,2,1,0:T(2,128)}), f32[256,3,2,128]{3,2,1,0:T(2,128)S(1)}, u32[]{:S(2)}, u32[]{:S(2)}) async-start(f32[256,3,2,128]{3,2,1,0:T(2,128)} %bitcast.17), calls=%async_computation.1 | async-start | bytes 1572864 | tf_op jit(solution)/shard_map/deliver_velocity/all_to_all | solution.py:341
  62.4 38.8 %collective-permute-start.4 = (f32[2,8,64,128]{3,2,1,0:T(8,128)S(1)}, f32[2,8,64,128]{3,2,1,0:T(8,128)S(1)}, u32[]{:S(2)}, u32[]{:S(2)}) collective-permute-start(f32[2,8,64,128]{3,2,1,0:T(8,128)S(1)} %halo_fields.3), channel_id=1, source_target_pairs={{0,1},{1,2},{2,3},{3,4},{4,5},{5,6},{6,7},{7,8},{8,9},{9,10},{10,1... | collective-permute-start | bytes 1572872 | tf_op jit(solution)/shard_map/halo_fields/ppermute | solution.py:312
  65.2 38.4 %collective-permute-start.5 = (f32[2,8,64,128]{3,2,1,0:T(8,128)S(1)}, f32[2,8,64,128]{3,2,1,0:T(8,128)S(1)}, u32[]{:S(2)}, u32[]{:S(2)}) collective-permute-start(f32[2,8,64,128]{3,2,1,0:T(8,128)S(1)} %halo_fields.3), channel_id=1, source_target_pairs={{1,0},{2,1},{3,2},{4,3},{5,4},{6,5},{7,6},{8,7},{9,8},{10,9},{11,1... | collective-permute-start | bytes 1572872 | tf_op jit(solution)/shard_map/halo_fields/ppermute | solution.py:312
  88.6 1.0 copy-start.8
  89.6 1.0 copy-start.10
  95.5 8.1 %collective-permute-start.2 = (f32[8,256]{1,0:T(8,128)S(1)}, f32[8,256]{1,0:T(8,128)S(1)}, u32[]{:S(2)}, u32[]{:S(2)}) collective-permute-start(f32[8,256]{1,0:T(8,128)S(1)} %get-tuple-element.13.ro), channel_id=1, source_target_pairs={{0,1},{1,2},{2,3},{3,4},{4,5},{5,6},{6,7},{7,8},{8,9},{9,10},{10,1... | collective-permute-start | bytes 24584 | tf_op jit(solution)/shard_map/residuals/ppermute | solution.py:312
  97.2 6.6 %collective-permute-start.3 = (f32[8,256]{1,0:T(8,128)S(1)}, f32[8,256]{1,0:T(8,128)S(1)}, u32[]{:S(2)}, u32[]{:S(2)}) collective-permute-start(f32[8,256]{1,0:T(8,128)S(1)} %get-tuple-element.13.ro), channel_id=1, source_target_pairs={{1,0},{2,1},{3,2},{4,3},{5,4},{6,5},{7,6},{8,7},{9,8},{10,9},{11,1... | collective-permute-start | bytes 24584 | tf_op jit(solution)/shard_map/residuals/ppermute | solution.py:312
  109.3 27.5 %all-to-all-start.2 = ((f32[256,2,128]{2,1,0:T(2,128)}), f32[256,2,128]{2,1,0:T(2,128)S(1)}, u32[]{:S(2)}, u32[]{:S(2)}) async-start(f32[256,2,128]{2,1,0:T(2,128)} %bitcast.21), calls=%async_computation.2 | async-start | bytes 524288 | tf_op jit(solution)/shard_map/spread_gradient/all_to_all | solution.py:355

commit v3 on v2

--- a/solution.py
+++ b/solution.py
@@ -1,3 +1,5 @@
+import functools
+
 import jax
 import jax.numpy as jnp
 from jax import lax
@@ -29,23 +31,29 @@
     return total
 
 
-def pick_kernel(index_ref, x_ref, out_ref):
-    rows = x_ref.shape[0]
-    index = index_ref[...]
-    onehot = (lax.broadcasted_iota(jnp.int32, (rows, index.shape[1]), 0) == index).astype(jnp.bfloat16)
-    out_ref[...] = dot3(onehot, x_ref[...], ((0,), (0,)))
-
-
-def drop_kernel(index_ref, x_ref, out_ref):
-    rows = out_ref.shape[0]
-    index = index_ref[...]
-    onehot = (lax.broadcasted_iota(jnp.int32, (rows, index.shape[1]), 0) == index).astype(jnp.bfloat16)
-    out_ref[...] = dot3(onehot, x_ref[...], ((1,), (0,)))
-
-
-def each(lo, hi, body):
-    for x in range(lo, hi):
-        body(x, 0)
+def paired(ref):
+    n = ref.shape[0] // 2
+    return jnp.concatenate([ref[pl.ds(0, n, stride=2), :], ref[pl.ds(1, n, stride=2), :]], axis=1)
+
+
+def pick_kernel(near_ref, x_ref, out_ref):
+    x = paired(x_ref)
+    n = near_ref.shape[1] // 2
+    near = lax.shift_right_arithmetic(near_ref[:, 0:n], 1)
+    onehot = (lax.broadcasted_iota(jnp.int32, (x.shape[0], n), 0) == near).astype(jnp.bfloat16)
+    picked = dot3(onehot, x, ((0,), (0,)))
+    for half in range(2):
+        out_ref[pl.ds(half, n, stride=2), :] = picked[:, half * LANES : (half + 1) * LANES]
+
+
+def drop_kernel(wanted_ref, x_ref, out_ref):
+    x = paired(x_ref)
+    wanted = wanted_ref[...]
+    slots = out_ref.shape[0] // 2
+    onehot = (lax.broadcasted_iota(jnp.int32, (slots, wanted.shape[1]), 0) == wanted).astype(jnp.bfloat16)
+    total = dot3(onehot, x, ((1,), (0,)))
+    for half in range(2):
+        out_ref[pl.ds(half, slots, stride=2), :] = total[:, half * LANES : (half + 1) * LANES]
 
 
 def tile_half(speed3, block, half, ny):
@@ -62,11 +70,28 @@
             dst[first : first + T // 2] = value * value
 
 
-def load_field(dst, edge_ref, low, own, high):
-    ny = own.shape[1]
-    dst[0:T, PADY : PADY + ny, :] = jnp.where(edge_ref[0] > 0, low[...], 0.0)
-    dst[T : 2 * T, PADY : PADY + ny, :] = own[...]
-    dst[2 * T : 3 * T, PADY : PADY + ny, :] = jnp.where(edge_ref[1] > 0, high[...], 0.0)
+def each(lo, hi, body):
+    for x in range(lo, hi):
+        body(x, 0)
+
+
+def bring(parts, ny, sems):
+    copies = []
+    for i, (src, dst, at) in enumerate(parts):
+        place = dst.at[at : at + src.shape[0], PADY : PADY + ny, :]
+        copies.append(pltpu.make_async_copy(src, place, sems.at[i]))
+    for c in copies:
+        c.start()
+    return copies
+
+
+def clear_edges(edge_ref, *fields):
+    for i, at in ((0, 0), (1, 2 * T)):
+
+        @pl.when(edge_ref[i] == 0)
+        def _():
+            for f in fields:
+                f[at : at + T] = jnp.zeros((T,) + f.shape[1:], jnp.float32)
 
 
 def clear_pad(dst, ny):
@@ -88,15 +113,24 @@
 def forward_kernel(
     edge_ref, src_ref, wave_ref, rec_ref, obs_ref,
     speed3, low, po, co, high,
-    lap_ref, res_ref, prev, cur, speed_sq,
+    lap_ref, res_ref, prev, cur, speed_sq, sems,
 ):
     ny = po.shape[1]
     rows = T * ny
     clear_pad(prev, ny)
     clear_pad(cur, ny)
-    load_field(prev, edge_ref, low.at[0], po, high.at[0])
-    load_field(cur, edge_ref, low.at[1], co, high.at[1])
+    copies = bring(
+        [
+            (low.at[0:T], prev, 0), (po, prev, T), (high.at[0:T], prev, 2 * T),
+            (low.at[T:], cur, 0), (co, cur, T), (high.at[T:], cur, 2 * T),
+        ],
+        ny,
+        sems,
+    )
     square_speed(speed_sq, speed3, ny)
+    for c in copies:
+        c.wait()
+    clear_edges(edge_ref, prev, cur)
     lane = lax.broadcasted_iota(jnp.int32, (ny, LANES), 1)
     first, last = lane == 0, lane == LANES - 1
     src_x, src_y, src_z = src_ref[0], src_ref[1], src_ref[2]
@@ -143,13 +177,19 @@
 def adjoint_kernel(
     edge_ref, rec_ref, rl, ro, rh,
     speed3, low, po, co, high, lap_ref,
-    out_ref, prev, cur, speed_sq, inject, speed,
+    out_ref, prev, cur, speed_sq, inject, speed, sems,
 ):
     ny = po.shape[1]
     clear_pad(prev, ny)
     clear_pad(cur, ny)
-    load_field(prev, edge_ref, low.at[0], po, high.at[0])
-    load_field(cur, edge_ref, low.at[1], co, high.at[1])
+    copies = bring(
+        [
+            (low.at[0:T], prev, 0), (po, prev, T), (high.at[0:T], prev, 2 * T),
+            (low.at[T:], cur, 0), (co, cur, T), (high.at[T:], cur, 2 * T),
+        ],
+        ny,
+        sems,
+    )
     square_speed(speed_sq, speed3, ny)
     lane = lax.broadcasted_iota(jnp.int32, (ny, LANES), 1)
     first, last = lane == 0, lane == LANES - 1
@@ -158,6 +198,9 @@
     rec = rec_ref[...]
     resid = rl[...] + ro[...] + rh[...]
     z_mask = lax.broadcasted_iota(jnp.int32, (LANES, REC), 0) == rec[1:2]
+    for c in copies:
+        c.wait()
+    clear_edges(edge_ref, prev, cur)
     for k in range(STEPS):
         old, now = (prev, cur) if k % 2 == 0 else (cur, prev)
         n = STEPS - 1 - k
@@ -203,18 +246,22 @@
     return pl.BlockSpec(memory_space=pltpu.SMEM)
 
 
+def anywhere():
+    return pl.BlockSpec(memory_space=pl.ANY)
+
+
 def params():
     return pltpu.CompilerParams(vmem_limit_bytes=48 * 1024 * 1024)
 
 
-def call_pick(index, x):
+def call_pick(near, x):
     return pl.pallas_call(
         pick_kernel,
-        out_shape=jax.ShapeDtypeStruct((index.shape[1], x.shape[1]), jnp.float32),
+        out_shape=jax.ShapeDtypeStruct((near.shape[1], x.shape[1]), jnp.float32),
         in_specs=[vmem(), vmem()],
         out_specs=vmem(),
         compiler_params=params(),
-    )(index, x)
+    )(near, x)
 
 
 def cut_kernel(x_ref, out_ref):
@@ -235,7 +282,7 @@
 
 def stack_kernel(*refs):
     fields, out, sems = refs[:-2], refs[-2], refs[-1]
-    copies = [pltpu.make_async_copy(f, out.at[i], sems.at[i]) for i, f in enumerate(fields)]
+    copies = [pltpu.make_async_copy(f, out.at[i * T : (i + 1) * T], sems.at[i]) for i, f in enumerate(fields)]
     for c in copies:
         c.start()
     for c in copies:
@@ -243,12 +290,11 @@
 
 
 def call_stack(*fields):
-    anywhere = pl.BlockSpec(memory_space=pl.ANY)
     return pl.pallas_call(
         stack_kernel,
-        out_shape=jax.ShapeDtypeStruct((len(fields),) + fields[0].shape, jnp.float32),
-        in_specs=[anywhere] * len(fields),
-        out_specs=anywhere,
+        out_shape=jax.ShapeDtypeStruct((len(fields) * T,) + fields[0].shape[1:], jnp.float32),
+        in_specs=[anywhere()] * len(fields),
+        out_specs=anywhere(),
         scratch_shapes=[pltpu.SemaphoreType.DMA((len(fields),))],
         compiler_params=params(),
     )(*fields)
@@ -264,9 +310,9 @@
             jax.ShapeDtypeStruct((STEPS, layers, ny, nz), jnp.float32),
             jax.ShapeDtypeStruct((STEPS, REC), jnp.float32),
         ),
-        in_specs=[smem()] * 3 + [vmem()] * 7,
+        in_specs=[smem()] * 3 + [vmem()] * 3 + [anywhere()] * 4,
         out_specs=(vmem(), vmem()),
-        scratch_shapes=[field, field, flat],
+        scratch_shapes=[field, field, flat, pltpu.SemaphoreType.DMA((6,))],
         compiler_params=params(),
     )(edge, src_place, wave, rec, obs, speed3, *fields)
 
@@ -278,9 +324,9 @@
     return pl.pallas_call(
         adjoint_kernel,
         out_shape=jax.ShapeDtypeStruct((layers, ny, nz), jnp.float32),
-        in_specs=[smem()] + [vmem()] * 10,
+        in_specs=[smem()] + [vmem()] * 5 + [anywhere()] * 4 + [vmem()],
         out_specs=vmem(),
-        scratch_shapes=[field, field, flat, flat, pltpu.VMEM((T, ny, nz), jnp.float32)],
+        scratch_shapes=[field, field, flat, flat, pltpu.VMEM((T, ny, nz), jnp.float32), pltpu.SemaphoreType.DMA((6,))],
         compiler_params=params(),
     )(edge, rec, *res3, speed3, *fields, laps)
 
@@ -314,13 +360,11 @@
     tiles = ((anchors[:, 0:1] + jnp.arange(n_sub, dtype=jnp.int32)) * n_shot + anchors[:, 1:2]).reshape(-1)
     table = jnp.arange(tile_slot.shape[0], dtype=jnp.int32)
     wanted = jnp.sum(jnp.where(table[:, None] == tiles[None, :], tile_slot[:, None], 0), axis=0)
-    want_rows = (wanted[:, None] * piece + jnp.arange(piece, dtype=jnp.int32)).reshape(1, n_all * piece)
-
     pad = jnp.pad(wanted.reshape(n_shot, n_sub), ((0, 0), (1, 1)), constant_values=-1)
     near = jnp.stack([pad[:, :-2], pad[:, 1:-1], pad[:, 2:]], axis=-1)
-    wide_rows = jnp.where(
-        near[..., None] >= 0, near[..., None] * piece + jnp.arange(piece, dtype=jnp.int32), -1
-    ).reshape(1, n_all * 3 * piece)
+    half = jnp.arange(piece, dtype=jnp.int32)[:, None, None, None]
+    near = jnp.where(near >= 0, near * piece + half, -1).reshape(1, n_all * 3 * piece)
+    wanted = wanted.reshape(1, n_all)
     edge = jnp.stack([sub_index > 0, sub_index < n_sub - 1]).astype(jnp.int32)
 
     cells = receiver_cells[0]
@@ -335,7 +379,7 @@
         cut = call_cut(velocity.reshape(local_slots * piece, n_all, nz))
         spread = lax.all_to_all(cut.reshape(n_all, local_slots, piece, nz), ALL, 0, 0, tiled=True)
     with jax.named_scope("pick_velocity"):
-        picked = call_pick(wide_rows, spread.reshape(n_all * local_slots * piece, nz))
+        picked = call_pick(near, spread.reshape(n_all * local_slots * piece, nz))
         picked, low, high = lax.optimization_barrier((picked, low, high))
     with jax.named_scope("deliver_velocity"):
         speed3 = lax.all_to_all(picked.reshape(n_all, 3, piece, nz), ALL, 0, 0, tiled=True)
@@ -360,7 +404,7 @@
             in_specs=[vmem(), vmem()],
             out_specs=vmem(),
             compiler_params=params(),
-        )(want_rows, pieces.reshape(n_all * piece, nz))
+        )(wanted, pieces.reshape(n_all * piece, nz))
     with jax.named_scope("deliver_gradient"):
         back = lax.all_to_all(dropped.reshape(n_all, local_slots * piece, nz), ALL, 0, 0, tiled=True)
         back = back.reshape(n_all, local_slots, piece, nz).transpose(1, 0, 2, 3)

time: 165 us -> 162 us (0.982)
  blocking collectives: 26.1 us -> 53.3 us
  waiting for transfers between devices: 59.3 us -> 44.8 us
  starting transfers between devices: 54 us -> 42.1 us
  Pallas kernels: 15.9 us -> 13.1 us
    all_to_all x0 -> x1, blocking collectives: none -> 27.2 us  [shards(): lax.all_to_all(image.reshape(n_all, piece, nz), ALL, 0, 0, tiled=True)]
    all_to_all x1 -> x0, waiting for transfers between devices: 15.1 us -> none  [shards(): lax.all_to_all(image.reshape(n_all, piece, nz), ALL, 0, 0, tiled=True)]
    all_to_all x1 -> x0, starting transfers between devices: 12.1 us -> none  [shards(): lax.all_to_all(image.reshape(n_all, piece, nz), ALL, 0, 0, tiled=True)]
    pallas_call x3, Pallas kernels: 3.71 us -> 1.9 us  [the longest x1 1.78 us: call_pick(): pl.pallas_call(pick_kernel, out_shape=jax.ShapeDtypeStruct((near.shape[1]...]
  transfers between devices with their start and end apart: 9 -> 8, of which waited for: 5 -> 4; matrix products, arithmetic and copies ran while one was open for 1% -> 1% of each run, Pallas kernels for 6% -> 5%
where the time goes in v3:
time: 162 us
  blocking collectives  53.3 us (33%)
  waiting for transfers between devices  44.8 us (28%)
  starting transfers between devices  42.1 us (26%)
  Pallas kernels  13.1 us (8%)
  local copies, waits for them, and re-layouts  7 us (4%)
    all_to_all x1, blocking collectives, shards(): lax.all_to_all(image.reshape(n_all, piece, nz), ALL, 0, 0, tiled=True)  27.2 us
    all_to_all x1, blocking collectives, shards(): lax.all_to_all(dropped.reshape(n_all, local_slots * piece, nz), ALL, 0, 0...  26.1 us
    all_to_all x1, waiting for transfers between devices, shards(): lax.all_to_all(cut.reshape(n_all, local_slots, piece, nz), ALL, 0, 0, til...  24.6 us
    ppermute x6, starting transfers between devices, both(): return (lax.ppermute(x, 'sub', forward), lax.ppermute(x, 'sub', backward))  22.4 us
    all_to_all x1, waiting for transfers between devices, shards(): lax.all_to_all(picked.reshape(n_all, 3, piece, nz), ALL, 0, 0, tiled=True)  17.9 us
    all_to_all x1, starting transfers between devices, shards(): lax.all_to_all(cut.reshape(n_all, local_slots, piece, nz), ALL, 0, 0, til...  10.7 us
    all_to_all x1, starting transfers between devices, shards(): lax.all_to_all(picked.reshape(n_all, 3, piece, nz), ALL, 0, 0, tiled=True)  9 us
    unnamed x32, local copies, waits for them, and re-layouts  5.1 us
  transfers between devices with their start and end apart: 8, of which 4 were waited for; matrix products, arithmetic and copies ran while one was open for 1% of the time, Pallas kernels for 5%

profile of v3, /device:TPU:1, one launch (start us, length us, event | category | flops | bytes accessed | tf_op | source)
XLA Modules:
  0.0 161.7 jit_solution(5770101297864259444)
XLA Ops:
  0.0 1.0 copy-done.2
  1.0 0.9 copy-done.4
  1.9 0.1 halo_fields.2
  2.0 3.9 %collective-permute-start = (f32[16,64,128]{2,1,0:T(8,128)S(1)}, f32[16,64,128]{2,1,0:T(8,128)S(1)}, u32[]{:S(2)}, u32[]{:S(2)}) collective-permute-start(f32[16,64,128]{2,1,0:T(8,128)S(1)} %halo_fields.2), channel_id=1, source_target_pairs={{0,1},{1,2},{2,3},{3,4},{4,5},{5,6},{6,7},{7,8},{8,9},{9,10},{10,1... | collective-permute-start | bytes 1572872 | tf_op jit(solution)/shard_map/halo_fields/ppermute | solution.py:358
  5.9 5.3 %collective-permute-start.1 = (f32[16,64,128]{2,1,0:T(8,128)S(1)}, f32[16,64,128]{2,1,0:T(8,128)S(1)}, u32[]{:S(2)}, u32[]{:S(2)}) collective-permute-start(f32[16,64,128]{2,1,0:T(8,128)S(1)} %halo_fields.2), channel_id=1, source_target_pairs={{1,0},{2,1},{3,2},{4,3},{5,4},{6,5},{7,6},{8,7},{9,8},{10,9},{11,1... | collective-permute-start | bytes 1572872 | tf_op jit(solution)/shard_map/halo_fields/ppermute | solution.py:358
  11.2 1.0 copy-done.6
  12.3 0.9 spread_velocity.1
  13.1 10.7 %all-to-all-start = ((f32[256,2,2,128]{3,2,1,0:T(2,128)}), f32[256,2,2,128]{3,2,1,0:T(2,128)S(1)}, u32[]{:S(2)}, u32[]{:S(2)}) async-start(f32[256,2,2,128]{3,2,1,0:T(2,128)} %bitcast.14), calls=%async_computation | async-start | bytes 1048576 | tf_op jit(solution)/shard_map/spread_velocity/all_to_all | solution.py:380
  23.8 0.0 copy-start
  23.8 0.0 copy-start.1
  23.8 0.1 multiply_add_fusion
  23.9 0.1 add.86
  24.0 0.2 select_reduce_fusion
  24.1 0.1 reshape.126
  24.2 0.1 stack.47
  24.3 0.1 slice_bitcast_fusion.1
  24.4 0.2 copy.18
  24.6 0.2 copy.17
  24.8 0.2 select_n.57.near_ref
  25.0 0.0 copy-start.14
  25.0 0.0 copy-start.3
  25.1 0.0 copy-start.5
  25.1 0.0 copy-start.11
  25.1 0.0 copy-start.12
  25.1 24.6 %all-to-all-done = f32[256,2,2,128]{3,2,1,0:T(2,128)S(1)} async-done(((f32[256,2,2,128]{3,2,1,0:T(2,128)}), f32[256,2,2,128]{3,2,1,0:T(2,128)S(1)}, u32[]{:S(2)}, u32[]{:S(2)}) %all-to-all-start) | async-done | bytes 524320 | tf_op jit(solution)/shard_map/spread_velocity/all_to_all | solution.py:380
  49.7 1.8 %pick_velocity.1 = f32[1536,128]{1,0:T(8,128)} custom-call(s32[1,1536]{1,0:T(1,128)S(1)} %select_n.57.near_ref, f32[1024,128]{1,0:T(8,128)S(1)} %bitcast.41), custom_call_target="tpu_custom_call" | custom-call | tf_op jit(solution)/shard_map/pick_velocity/pallas_call | solution.py:258
  51.5 0.0 collective-permute-done.low
  51.5 0.0 collective-permute-done.1.high
  51.5 9.0 %all-to-all-start.1 = ((f32[256,3,2,128]{3,2,1,0:T(2,128)}), f32[256,3,2,128]{3,2,1,0:T(2,128)S(1)}, u32[]{:S(2)}, u32[]{:S(2)}) async-start(f32[256,3,2,128]{3,2,1,0:T(2,128)} %bitcast.18), calls=%async_computation.1 | async-start | bytes 1572864 | tf_op jit(solution)/shard_map/deliver_velocity/all_to_all | solution.py:385
  60.5 0.1 halo_fields.3
  60.6 2.8 %collective-permute-start.4 = (f32[16,64,128]{2,1,0:T(8,128)S(1)}, f32[16,64,128]{2,1,0:T(8,128)S(1)}, u32[]{:S(2)}, u32[]{:S(2)}) collective-permute-start(f32[16,64,128]{2,1,0:T(8,128)S(1)} %halo_fields.3), channel_id=1, source_target_pairs={{0,1},{1,2},{2,3},{3,4},{4,5},{5,6},{6,7},{7,8},{8,9},{9,10},{10,1... | collective-permute-start | bytes 1572872 | tf_op jit(solution)/shard_map/halo_fields/ppermute | solution.py:358
  63.4 4.5 %collective-permute-start.5 = (f32[16,64,128]{2,1,0:T(8,128)S(1)}, f32[16,64,128]{2,1,0:T(8,128)S(1)}, u32[]{:S(2)}, u32[]{:S(2)}) collective-permute-start(f32[16,64,128]{2,1,0:T(8,128)S(1)} %halo_fields.3), channel_id=1, source_target_pairs={{1,0},{2,1},{3,2},{4,3},{5,4},{6,5},{7,6},{8,7},{9,8},{10,9},{11,1... | collective-permute-start | bytes 1572872 | tf_op jit(solution)/shard_map/halo_fields/ppermute | solution.py:358
  68.6 0.1 add_convert_fusion.edge_ref
  68.7 0.1 pad_add_fusion.2.src_ref
  68.8 17.9 %all-to-all-done.1 = f32[256,3,2,128]{3,2,1,0:T(2,128)S(1)} async-done(((f32[256,3,2,128]{3,2,1,0:T(2,128)}), f32[256,3,2,128]{3,2,1,0:T(2,128)S(1)}, u32[]{:S(2)}, u32[]{:S(2)}) %all-to-all-start.1) | async-done | bytes 786464 | tf_op jit(solution)/shard_map/deliver_velocity/all_to_all | solution.py:385
  86.7 0.0 copy-start.8
  86.8 1.0 copy-done.8
  87.8 1.0 copy-done.10
  88.8 4.9 %forward.1 = (f32[8,8,64,128]{3,2,1,0:T(8,128)S(1)}, f32[8,256]{1,0:T(8,128)S(1)}) custom-call(s32[2]{0:T(128)S(1)} %add_convert_fusion.edge_ref, s32[3]{0:T(128)S(1)} %pad_add_fusion.2.src_ref, f32[8]{0:T(128)S(1)} %bitcast.56, s32[2,256]{1,0:T(2,128)S(1)} %pad_add_fusion.1.rec_ref, f32[8,256]{1,0:T(8,128)S(1)} %bitcast.55, f32[1536,128]{1,0:T(8,128)S(1)} %bitcast.39, ...), custom_call_target="tpu_custom_call" | custom-call | tf_op jit(solution)/shard_map/forward/pallas_call | solution.py:307
  93.7 1.8 %collective-permute-start.2 = (f32[8,256]{1,0:T(8,128)S(1)}, f32[8,256]{1,0:T(8,128)S(1)}, u32[]{:S(2)}, u32[]{:S(2)}) collective-permute-start(f32[8,256]{1,0:T(8,128)S(1)} %get-tuple-element.13.ro), channel_id=1, source_target_pairs={{0,1},{1,2},{2,3},{3,4},{4,5},{5,6},{6,7},{7,8},{8,9},{9,10},{10,1... | collective-permute-start | bytes 24584 | tf_op jit(solution)/shard_map/residuals/ppermute | solution.py:358
  95.6 4.1 %collective-permute-start.3 = (f32[8,256]{1,0:T(8,128)S(1)}, f32[8,256]{1,0:T(8,128)S(1)}, u32[]{:S(2)}, u32[]{:S(2)}) collective-permute-start(f32[8,256]{1,0:T(8,128)S(1)} %get-tuple-element.13.ro), channel_id=1, source_target_pairs={{1,0},{2,1},{3,2},{4,3},{5,4},{6,5},{7,6},{8,7},{9,8},{10,9},{11,1... | collective-permute-start | bytes 24584 | tf_op jit(solution)/shard_map/residuals/ppermute | solution.py:358
  99.7 2.1 %collective-permute-done.5.high = f32[16,64,128]{2,1,0:T(8,128)S(1)} collective-permute-done((f32[16,64,128]{2,1,0:T(8,128)S(1)}, f32[16,64,128]{2,1,0:T(8,128)S(1)}, u32[]{:S(2)}, u32[]{:S(2)}) %collective-permute-start.5) | collective-permute-done | bytes 524320 | tf_op jit(solution)/shard_map/halo_fields/ppermute | solution.py:358
  101.8 0.2 collective-permute-done.3.rh
  101.9 5.0 %adjoint.1 = f32[8,64,128]{2,1,0:T(8,128)S(1)} custom-call(s32[2]{0:T(128)S(1)} %add_convert_fusion.edge_ref, s32[2,256]{1,0:T(2,128)S(1)} %pad_add_fusion.1.rec_ref, f32[8,256]{1,0:T(8,128)S(1)} %collective-permute-done.2.rl, f32[8,256]{1,0:T(8,128)S(1)} %get-tuple-element.13.ro, f32[8,256]{1,0:T(8,128)S(1)} %collective-permute-done.3.rh, ...), custom_call_target="tpu_custom_call" | custom-call | tf_op jit(solution)/shard_map/adjoint/pallas_call | solution.py:324
  107.0 27.2 %all_to_all.20 = f32[256,2,128]{2,1,0:T(2,128)S(1)} all-to-all(f32[256,2,128]{2,1,0:T(2,128)S(1)} %bitcast.43), channel_id=1, replica_groups=mesh['shot'=16,'sub'=16] {'shot','sub'}, dimensions={0} | all-to-all | bytes 524288 | tf_op jit(solution)/shard_map/spread_gradient/all_to_all | solution.py:399
  134.2 0.4 drop_gradient.1
  134.6 26.1 %all_to_all.21 = f32[256,4,128]{2,1,0:T(4,128)S(1)} all-to-all(f32[256,4,128]{2,1,0:T(4,128)S(1)} %bitcast.42), channel_id=1, replica_groups=mesh['shot'=16,'sub'=16] {'shot','sub'}, dimensions={0} | all-to-all | bytes 1048576 | tf_op jit(solution)/shard_map/deliver_gradient/all_to_all | solution.py:409
  160.7 1.0 copy.19
  (27 shorter events, 0.1 us)
Async XLA Ops:
  0.0 23.8 %copy-start.15 = (s32[16,2]{0,1:T(2,128)S(1)}, s32[16,2]{0,1:T(2,128)}, u32[]{:S(2)}) copy-start(s32[16,2]{0,1:T(2,128)} %param.13) | copy-start | bytes 388
  0.0 24.0 %copy-start.13 = (s32[512]{0:T(512)S(1)}, s32[512]{0:T(512)}, u32[]{:S(2)}) copy-start(s32[512]{0:T(512)} %param.12) | copy-start | bytes 6148
  0.0 1.0 copy-start.2
  1.0 0.9 copy-start.4
  2.0 49.5 %collective-permute-start = (f32[16,64,128]{2,1,0:T(8,128)S(1)}, f32[16,64,128]{2,1,0:T(8,128)S(1)}, u32[]{:S(2)}, u32[]{:S(2)}) collective-permute-start(f32[16,64,128]{2,1,0:T(8,128)S(1)} %halo_fields.2), channel_id=1, source_target_pairs={{0,1},{1,2},{2,3},{3,4},{4,5},{5,6},{6,7},{7,8},{8,9},{9,10},{10,1... | collective-permute-start | bytes 1572872 | tf_op jit(solution)/shard_map/halo_fields/ppermute | solution.py:358
  5.9 45.6 %collective-permute-start.1 = (f32[16,64,128]{2,1,0:T(8,128)S(1)}, f32[16,64,128]{2,1,0:T(8,128)S(1)}, u32[]{:S(2)}, u32[]{:S(2)}) collective-permute-start(f32[16,64,128]{2,1,0:T(8,128)S(1)} %halo_fields.2), channel_id=1, source_target_pairs={{1,0},{2,1},{3,2},{4,3},{5,4},{6,5},{7,6},{8,7},{9,8},{10,9},{11,1... | collective-permute-start | bytes 1572872 | tf_op jit(solution)/shard_map/halo_fields/ppermute | solution.py:358
  11.2 1.0 copy-start.6
  13.1 36.6 %all-to-all-start = ((f32[256,2,2,128]{3,2,1,0:T(2,128)}), f32[256,2,2,128]{3,2,1,0:T(2,128)S(1)}, u32[]{:S(2)}, u32[]{:S(2)}) async-start(f32[256,2,2,128]{3,2,1,0:T(2,128)} %bitcast.14), calls=%async_computation | async-start | bytes 1048576 | tf_op jit(solution)/shard_map/spread_velocity/all_to_all | solution.py:380
  23.8 36.7 %copy-start = (f32[1,8,64,128]{3,2,1,0:T(8,128)S(1)}, f32[1,8,64,128]{3,2,1,0:T(8,128)}, u32[]{:S(2)}) copy-start(f32[1,8,64,128]{3,2,1,0:T(8,128)} %param.20) | copy-start | bytes 786436
  23.8 36.7 %copy-start.1 = (f32[1,8,64,128]{3,2,1,0:T(8,128)S(1)}, f32[1,8,64,128]{3,2,1,0:T(8,128)}, u32[]{:S(2)}) copy-start(f32[1,8,64,128]{3,2,1,0:T(8,128)} %param.21) | copy-start | bytes 786436
  25.0 43.7 %copy-start.14 = (s32[1,256]{1,0:T(1,128)S(1)}, s32[1,256]{1,0:T(1,128)}, u32[]{:S(2)}) copy-start(s32[1,256]{1,0:T(1,128)} %param.16) | copy-start | bytes 3076
  25.0 61.7 %copy-start.3 = (f32[1,8,64,128]{3,2,1,0:T(8,128)S(1)}, f32[1,8,64,128]{3,2,1,0:T(8,128)}, u32[]{:S(2)}) copy-start(f32[1,8,64,128]{3,2,1,0:T(8,128)} %param.18) | copy-start | bytes 786436
  25.1 61.7 %copy-start.5 = (f32[1,8,64,128]{3,2,1,0:T(8,128)S(1)}, f32[1,8,64,128]{3,2,1,0:T(8,128)}, u32[]{:S(2)}) copy-start(f32[1,8,64,128]{3,2,1,0:T(8,128)} %param.19) | copy-start | bytes 786436
  25.1 61.7 %copy-start.11 = (f32[1,8,256]{2,1,0:T(8,128)S(1)}, f32[1,8,256]{2,1,0:T(8,128)}, u32[]{:S(2)}) copy-start(f32[1,8,256]{2,1,0:T(8,128)} %param.17) | copy-start | bytes 24580
  25.1 61.7 %copy-start.12 = (f32[1,8]{1,0:T(1,128)S(1)}, f32[1,8]{1,0:T(1,128)}, u32[]{:S(2)}) copy-start(f32[1,8]{1,0:T(1,128)} %param.15) | copy-start | bytes 100
  51.5 9.1 %copy-start.7 = (f32[16,64,128]{2,1,0:T(8,128)}, f32[16,64,128]{2,1,0:T(8,128)S(1)}, u32[]{:S(2)}) copy-start(f32[16,64,128]{2,1,0:T(8,128)S(1)} %collective-permute-done.low) | copy-start | bytes 1572868
  51.5 9.0 %copy-start.9 = (f32[16,64,128]{2,1,0:T(8,128)}, f32[16,64,128]{2,1,0:T(8,128)S(1)}, u32[]{:S(2)}) copy-start(f32[16,64,128]{2,1,0:T(8,128)S(1)} %collective-permute-done.1.high) | copy-start | bytes 1572868
  51.5 35.2 %all-to-all-start.1 = ((f32[256,3,2,128]{3,2,1,0:T(2,128)}), f32[256,3,2,128]{3,2,1,0:T(2,128)S(1)}, u32[]{:S(2)}, u32[]{:S(2)}) async-start(f32[256,3,2,128]{3,2,1,0:T(2,128)} %bitcast.18), calls=%async_computation.1 | async-start | bytes 1572864 | tf_op jit(solution)/shard_map/deliver_velocity/all_to_all | solution.py:385
  60.6 39.1 %collective-permute-start.4 = (f32[16,64,128]{2,1,0:T(8,128)S(1)}, f32[16,64,128]{2,1,0:T(8,128)S(1)}, u32[]{:S(2)}, u32[]{:S(2)}) collective-permute-start(f32[16,64,128]{2,1,0:T(8,128)S(1)} %halo_fields.3), channel_id=1, source_target_pairs={{0,1},{1,2},{2,3},{3,4},{4,5},{5,6},{6,7},{7,8},{8,9},{9,10},{10,1... | collective-permute-start | bytes 1572872 | tf_op jit(solution)/shard_map/halo_fields/ppermute | solution.py:358
  63.4 38.4 %collective-permute-start.5 = (f32[16,64,128]{2,1,0:T(8,128)S(1)}, f32[16,64,128]{2,1,0:T(8,128)S(1)}, u32[]{:S(2)}, u32[]{:S(2)}) collective-permute-start(f32[16,64,128]{2,1,0:T(8,128)S(1)} %halo_fields.3), channel_id=1, source_target_pairs={{1,0},{2,1},{3,2},{4,3},{5,4},{6,5},{7,6},{8,7},{9,8},{10,9},{11,1... | collective-permute-start | bytes 1572872 | tf_op jit(solution)/shard_map/halo_fields/ppermute | solution.py:358
  86.7 1.0 copy-start.8
  87.8 1.0 copy-start.10
  93.7 8.0 %collective-permute-start.2 = (f32[8,256]{1,0:T(8,128)S(1)}, f32[8,256]{1,0:T(8,128)S(1)}, u32[]{:S(2)}, u32[]{:S(2)}) collective-permute-start(f32[8,256]{1,0:T(8,128)S(1)} %get-tuple-element.13.ro), channel_id=1, source_target_pairs={{0,1},{1,2},{2,3},{3,4},{4,5},{5,6},{6,7},{7,8},{8,9},{9,10},{10,1... | collective-permute-start | bytes 24584 | tf_op jit(solution)/shard_map/residuals/ppermute | solution.py:358
  95.6 6.4 %collective-permute-start.3 = (f32[8,256]{1,0:T(8,128)S(1)}, f32[8,256]{1,0:T(8,128)S(1)}, u32[]{:S(2)}, u32[]{:S(2)}) collective-permute-start(f32[8,256]{1,0:T(8,128)S(1)} %get-tuple-element.13.ro), channel_id=1, source_target_pairs={{1,0},{2,1},{3,2},{4,3},{5,4},{6,5},{7,6},{8,7},{9,8},{10,9},{11,1... | collective-permute-start | bytes 24584 | tf_op jit(solution)/shard_map/residuals/ppermute | solution.py:358

commit v4 on v3

--- a/solution.py
+++ b/solution.py
@@ -184,8 +184,8 @@
     clear_pad(cur, ny)
     copies = bring(
         [
-            (low.at[0:T], prev, 0), (po, prev, T), (high.at[0:T], prev, 2 * T),
-            (low.at[T:], cur, 0), (co, cur, T), (high.at[T:], cur, 2 * T),
+            (low.at[0 : T - 1], prev, 1), (po, prev, T), (high.at[0 : T - 1], prev, 2 * T),
+            (low.at[T - 1 :], cur, 0), (co, cur, T), (high.at[T - 1 :], cur, 2 * T),
         ],
         ny,
         sems,
@@ -280,19 +280,23 @@
     )(x)
 
 
-def stack_kernel(*refs):
+def stack_kernel(first, count, *refs):
     fields, out, sems = refs[:-2], refs[-2], refs[-1]
-    copies = [pltpu.make_async_copy(f, out.at[i * T : (i + 1) * T], sems.at[i]) for i, f in enumerate(fields)]
+    copies = []
+    for i, field in enumerate(fields):
+        at, part = (0, field.at[first : first + count]) if i == 0 else (count + (i - 1) * T, field)
+        copies.append(pltpu.make_async_copy(part, out.at[at : at + part.shape[0]], sems.at[i]))
     for c in copies:
         c.start()
     for c in copies:
         c.wait()
 
 
-def call_stack(*fields):
+def call_stack(first, count, *fields):
+    layers = count + (len(fields) - 1) * T
     return pl.pallas_call(
-        stack_kernel,
-        out_shape=jax.ShapeDtypeStruct((len(fields) * T,) + fields[0].shape[1:], jnp.float32),
+        functools.partial(stack_kernel, first, count),
+        out_shape=jax.ShapeDtypeStruct((layers,) + fields[0].shape[1:], jnp.float32),
         in_specs=[anywhere()] * len(fields),
         out_specs=anywhere(),
         scratch_shapes=[pltpu.SemaphoreType.DMA((len(fields),))],
@@ -354,8 +358,8 @@
     forward = [(i, (i + 1) % n_sub) for i in range(n_sub)]
     backward = [(j, i) for i, j in forward]
 
-    def both(x):
-        return lax.ppermute(x, "sub", forward), lax.ppermute(x, "sub", backward)
+    def both(up, down):
+        return lax.ppermute(up, "sub", forward), lax.ppermute(down, "sub", backward)
 
     tiles = ((anchors[:, 0:1] + jnp.arange(n_sub, dtype=jnp.int32)) * n_shot + anchors[:, 1:2]).reshape(-1)
     table = jnp.arange(tile_slot.shape[0], dtype=jnp.int32)
@@ -373,8 +377,8 @@
     src_place = jnp.stack([src // (ny * nz) - (sub_index - 1) * layers, src // nz % ny, src % nz])
 
     with jax.named_scope("halo_fields"):
-        low, high = both(call_stack(fwd_prev[0], fwd_curr[0]))
-        adj_low, adj_high = both(call_stack(adj_prev[0], adj_curr[0]))
+        low, high = both(*[call_stack(0, T, fwd_prev[0], fwd_curr[0])] * 2)
+        adj_low, adj_high = both(*(call_stack(first, T - 1, adj_prev[0], adj_curr[0]) for first in (1, 0)))
     with jax.named_scope("spread_velocity"):
         cut = call_cut(velocity.reshape(local_slots * piece, n_all, nz))
         spread = lax.all_to_all(cut.reshape(n_all, local_slots, piece, nz), ALL, 0, 0, tiled=True)
@@ -390,7 +394,7 @@
     with jax.named_scope("forward"):
         laps, resid = call_forward(edge, src_place, wavelet[0], rec, observed[0], speed3, fwd4)
     with jax.named_scope("residuals"):
-        res_low, res_high = both(resid)
+        res_low, res_high = both(resid, resid)
         res3 = (res_low, resid, res_high)
     with jax.named_scope("adjoint"):
         image = call_adjoint(edge, rec, res3, speed3, adj4, laps)

time: 162 us -> 162 us (level)
  Pallas kernels: 13.1 us -> 15.6 us
  local copies, waits for them, and re-layouts: 7 us -> 4.9 us
    unnamed x32 -> x24, local copies, waits for them, and re-layouts: 5.1 us -> 3.01 us
  transfers between devices with their start and end apart: 8 -> 8, of which waited for: 4 -> 4; matrix products, arithmetic and copies ran while one was open for 1% -> 1% of each run, Pallas kernels for 5% -> 6%
where the time goes in v4:
time: 162 us; the launch traced here: 161 us
  blocking collectives  53.3 us (33%)
  waiting for transfers between devices  44.1 us (27%)
  starting transfers between devices  42.1 us (26%)
  Pallas kernels  15.6 us (10%)
  local copies, waits for them, and re-layouts  4.9 us (3%)
    all_to_all x1, blocking collectives, shards(): lax.all_to_all(image.reshape(n_all, piece, nz), ALL, 0, 0, tiled=True)  27.1 us
    all_to_all x1, blocking collectives, shards(): lax.all_to_all(dropped.reshape(n_all, local_slots * piece, nz), ALL, 0, 0...  26.1 us
    all_to_all x1, waiting for transfers between devices, shards(): lax.all_to_all(cut.reshape(n_all, local_slots, piece, nz), ALL, 0, 0, til...  24.7 us
    all_to_all x1, waiting for transfers between devices, shards(): lax.all_to_all(picked.reshape(n_all, 3, piece, nz), ALL, 0, 0, tiled=True)  16.4 us
    ppermute x3, starting transfers between devices, both(): lax.ppermute(down, 'sub', backward)  14 us
    all_to_all x1, starting transfers between devices, shards(): lax.all_to_all(cut.reshape(n_all, local_slots, piece, nz), ALL, 0, 0, til...  10.7 us
    all_to_all x1, starting transfers between devices, shards(): lax.all_to_all(picked.reshape(n_all, 3, piece, nz), ALL, 0, 0, tiled=True)  9 us
    ppermute x3, starting transfers between devices, both(): lax.ppermute(up, 'sub', forward)  8.46 us
  transfers between devices with their start and end apart: 8, of which 4 were waited for; matrix products, arithmetic and copies ran while one was open for 1% of the time, Pallas kernels for 6%

profile of v4, /device:TPU:1, one launch (start us, length us, event | category | flops | bytes accessed | tf_op | source)
XLA Modules:
  0.0 161.3 jit_solution(5692285577785652219)
XLA Ops:
  0.0 1.0 copy-done.2
  1.0 0.9 copy-done.4
  1.9 0.1 halo_fields.3
  2.0 3.9 %collective-permute-start = (f32[16,64,128]{2,1,0:T(8,128)S(1)}, f32[16,64,128]{2,1,0:T(8,128)S(1)}, u32[]{:S(2)}, u32[]{:S(2)}) collective-permute-start(f32[16,64,128]{2,1,0:T(8,128)S(1)} %halo_fields.3), channel_id=1, source_target_pairs={{0,1},{1,2},{2,3},{3,4},{4,5},{5,6},{6,7},{7,8},{8,9},{9,10},{10,1... | collective-permute-start | bytes 1572872 | tf_op jit(solution)/shard_map/halo_fields/ppermute | solution.py:362
  5.9 5.3 %collective-permute-start.1 = (f32[16,64,128]{2,1,0:T(8,128)S(1)}, f32[16,64,128]{2,1,0:T(8,128)S(1)}, u32[]{:S(2)}, u32[]{:S(2)}) collective-permute-start(f32[16,64,128]{2,1,0:T(8,128)S(1)} %halo_fields.3), channel_id=1, source_target_pairs={{1,0},{2,1},{3,2},{4,3},{5,4},{6,5},{7,6},{8,7},{9,8},{10,9},{11,1... | collective-permute-start | bytes 1572872 | tf_op jit(solution)/shard_map/halo_fields/ppermute | solution.py:362
  11.2 1.0 copy-done.6
  12.3 0.9 spread_velocity.1
  13.1 10.7 %all-to-all-start = ((f32[256,2,2,128]{3,2,1,0:T(2,128)}), f32[256,2,2,128]{3,2,1,0:T(2,128)S(1)}, u32[]{:S(2)}, u32[]{:S(2)}) async-start(f32[256,2,2,128]{3,2,1,0:T(2,128)} %bitcast.14), calls=%async_computation | async-start | bytes 1048576 | tf_op jit(solution)/shard_map/spread_velocity/all_to_all | solution.py:384
  23.8 0.0 copy-done.11
  23.8 0.0 copy-start
  23.8 0.0 copy-start.1
  23.8 0.1 multiply_add_fusion
  23.9 0.1 add.86
  24.0 0.2 select_reduce_fusion
  24.1 0.1 reshape.126
  24.2 0.1 stack.47
  24.3 0.1 slice_bitcast_fusion.1
  24.4 0.2 copy.18
  24.6 0.2 copy.17
  24.8 0.2 select_n.57.near_ref
  25.0 24.7 %all-to-all-done = f32[256,2,2,128]{3,2,1,0:T(2,128)S(1)} async-done(((f32[256,2,2,128]{3,2,1,0:T(2,128)}), f32[256,2,2,128]{3,2,1,0:T(2,128)S(1)}, u32[]{:S(2)}, u32[]{:S(2)}) %all-to-all-start) | async-done | bytes 524320 | tf_op jit(solution)/shard_map/spread_velocity/all_to_all | solution.py:384
  49.7 1.8 %pick_velocity.1 = f32[1536,128]{1,0:T(8,128)} custom-call(s32[1,1536]{1,0:T(1,128)S(1)} %select_n.57.near_ref, f32[1024,128]{1,0:T(8,128)S(1)} %bitcast.47), custom_call_target="tpu_custom_call" | custom-call | tf_op jit(solution)/shard_map/pick_velocity/pallas_call | solution.py:258
  51.5 0.0 copy-start.8
  51.5 0.0 collective-permute-done.low
  51.5 0.0 collective-permute-done.1.high
  51.5 9.0 %all-to-all-start.1 = ((f32[256,3,2,128]{3,2,1,0:T(2,128)}), f32[256,3,2,128]{3,2,1,0:T(2,128)S(1)}, u32[]{:S(2)}, u32[]{:S(2)}) async-start(f32[256,3,2,128]{3,2,1,0:T(2,128)} %bitcast.18), calls=%async_computation.1 | async-start | bytes 1572864 | tf_op jit(solution)/shard_map/deliver_velocity/all_to_all | solution.py:389
  60.5 0.0 copy-done
  60.5 0.0 copy-done.1
  60.5 0.8 halo_fields.4
  61.4 2.8 %collective-permute-start.4 = (f32[15,64,128]{2,1,0:T(8,128)}, f32[15,64,128]{2,1,0:T(8,128)S(1)}, u32[]{:S(2)}, u32[]{:S(2)}) collective-permute-start(f32[15,64,128]{2,1,0:T(8,128)} %halo_fields.4), channel_id=1, source_target_pairs={{0,1},{1,2},{2,3},{3,4},{4,5},{5,6},{6,7},{7,8},{8,9},{9,10},{10,1... | collective-permute-start | bytes 1474568 | tf_op jit(solution)/shard_map/halo_fields/ppermute | solution.py:362
  64.1 0.8 halo_fields.5
  64.9 4.5 %collective-permute-start.5 = (f32[15,64,128]{2,1,0:T(8,128)}, f32[15,64,128]{2,1,0:T(8,128)}, u32[]{:S(2)}, u32[]{:S(2)}) collective-permute-start(f32[15,64,128]{2,1,0:T(8,128)} %halo_fields.5), channel_id=1, source_target_pairs={{1,0},{2,1},{3,2},{4,3},{5,4},{6,5},{7,6},{8,7},{9,8},{10,9},{11,1... | collective-permute-start | bytes 1474568 | tf_op jit(solution)/shard_map/halo_fields/ppermute | solution.py:362
  69.5 0.1 add_convert_fusion.edge_ref
  70.2 0.1 pad_add_fusion.2.src_ref
  70.3 0.0 copy-done.10
  70.4 16.4 %all-to-all-done.1 = f32[256,3,2,128]{3,2,1,0:T(2,128)S(1)} async-done(((f32[256,3,2,128]{3,2,1,0:T(2,128)}), f32[256,3,2,128]{3,2,1,0:T(2,128)S(1)}, u32[]{:S(2)}, u32[]{:S(2)}) %all-to-all-start.1) | async-done | bytes 786464 | tf_op jit(solution)/shard_map/deliver_velocity/all_to_all | solution.py:389
  86.8 4.9 %forward.1 = (f32[8,8,64,128]{3,2,1,0:T(8,128)S(1)}, f32[8,256]{1,0:T(8,128)S(1)}) custom-call(s32[2]{0:T(128)S(1)} %add_convert_fusion.edge_ref, s32[3]{0:T(128)S(1)} %pad_add_fusion.2.src_ref, f32[8]{0:T(128)S(1)} %bitcast.58, s32[2,256]{1,0:T(2,128)S(1)} %pad_add_fusion.1.rec_ref, f32[8,256]{1,0:T(8,128)S(1)} %bitcast.57, f32[1536,128]{1,0:T(8,128)S(1)} %bitcast.39, ...), custom_call_target="tpu_custom_call" | custom-call | tf_op jit(solution)/shard_map/forward/pallas_call | solution.py:311
  91.7 1.8 %collective-permute-start.2 = (f32[8,256]{1,0:T(8,128)S(1)}, f32[8,256]{1,0:T(8,128)S(1)}, u32[]{:S(2)}, u32[]{:S(2)}) collective-permute-start(f32[8,256]{1,0:T(8,128)S(1)} %get-tuple-element.13.ro), channel_id=1, source_target_pairs={{0,1},{1,2},{2,3},{3,4},{4,5},{5,6},{6,7},{7,8},{8,9},{9,10},{10,1... | collective-permute-start | bytes 24584 | tf_op jit(solution)/shard_map/residuals/ppermute | solution.py:362
  93.5 4.1 %collective-permute-start.3 = (f32[8,256]{1,0:T(8,128)S(1)}, f32[8,256]{1,0:T(8,128)S(1)}, u32[]{:S(2)}, u32[]{:S(2)}) collective-permute-start(f32[8,256]{1,0:T(8,128)S(1)} %get-tuple-element.13.ro), channel_id=1, source_target_pairs={{1,0},{2,1},{3,2},{4,3},{5,4},{6,5},{7,6},{8,7},{9,8},{10,9},{11,1... | collective-permute-start | bytes 24584 | tf_op jit(solution)/shard_map/residuals/ppermute | solution.py:362
  97.6 0.0 collective-permute-done.4.low
  97.6 2.9 %collective-permute-done.5.high = f32[15,64,128]{2,1,0:T(8,128)} collective-permute-done((f32[15,64,128]{2,1,0:T(8,128)}, f32[15,64,128]{2,1,0:T(8,128)}, u32[]{:S(2)}, u32[]{:S(2)}) %collective-permute-start.5) | collective-permute-done | bytes 491552 | tf_op jit(solution)/shard_map/halo_fields/ppermute | solution.py:362
  100.5 0.0 collective-permute-done.2.rl
  100.5 0.2 collective-permute-done.3.rh
  100.7 6.0 %adjoint.1 = f32[8,64,128]{2,1,0:T(8,128)S(1)} custom-call(s32[2]{0:T(128)S(1)} %add_convert_fusion.edge_ref, s32[2,256]{1,0:T(2,128)S(1)} %pad_add_fusion.1.rec_ref, f32[8,256]{1,0:T(8,128)S(1)} %collective-permute-done.2.rl, f32[8,256]{1,0:T(8,128)S(1)} %get-tuple-element.13.ro, f32[8,256]{1,0:T(8,128)S(1)} %collective-permute-done.3.rh, ...), custom_call_target="tpu_custom_call" | custom-call | tf_op jit(solution)/shard_map/adjoint/pallas_call | solution.py:328
  106.7 27.1 %all_to_all.20 = f32[256,2,128]{2,1,0:T(2,128)S(1)} all-to-all(f32[256,2,128]{2,1,0:T(2,128)S(1)} %bitcast.49), channel_id=1, replica_groups=mesh['shot'=16,'sub'=16] {'shot','sub'}, dimensions={0} | all-to-all | bytes 524288 | tf_op jit(solution)/shard_map/spread_gradient/all_to_all | solution.py:403
  133.8 0.4 drop_gradient.1
  134.2 26.1 %all_to_all.21 = f32[256,4,128]{2,1,0:T(4,128)S(1)} all-to-all(f32[256,4,128]{2,1,0:T(4,128)S(1)} %bitcast.48), channel_id=1, replica_groups=mesh['shot'=16,'sub'=16] {'shot','sub'}, dimensions={0} | all-to-all | bytes 1048576 | tf_op jit(solution)/shard_map/deliver_gradient/all_to_all | solution.py:413
  160.3 1.0 copy.19
  (20 shorter events, 0.1 us)
Async XLA Ops:
  0.0 23.8 %copy-start.11 = (s32[16,2]{0,1:T(2,128)S(1)}, s32[16,2]{0,1:T(2,128)}, u32[]{:S(2)}) copy-start(s32[16,2]{0,1:T(2,128)} %param.13) | copy-start | bytes 388
  0.0 24.0 %copy-start.9 = (s32[512]{0:T(512)S(1)}, s32[512]{0:T(512)}, u32[]{:S(2)}) copy-start(s32[512]{0:T(512)} %param.12) | copy-start | bytes 6148
  0.0 1.0 copy-start.2
  1.0 0.9 copy-start.4
  2.0 49.5 %collective-permute-start = (f32[16,64,128]{2,1,0:T(8,128)S(1)}, f32[16,64,128]{2,1,0:T(8,128)S(1)}, u32[]{:S(2)}, u32[]{:S(2)}) collective-permute-start(f32[16,64,128]{2,1,0:T(8,128)S(1)} %halo_fields.3), channel_id=1, source_target_pairs={{0,1},{1,2},{2,3},{3,4},{4,5},{5,6},{6,7},{7,8},{8,9},{9,10},{10,1... | collective-permute-start | bytes 1572872 | tf_op jit(solution)/shard_map/halo_fields/ppermute | solution.py:362
  5.9 45.6 %collective-permute-start.1 = (f32[16,64,128]{2,1,0:T(8,128)S(1)}, f32[16,64,128]{2,1,0:T(8,128)S(1)}, u32[]{:S(2)}, u32[]{:S(2)}) collective-permute-start(f32[16,64,128]{2,1,0:T(8,128)S(1)} %halo_fields.3), channel_id=1, source_target_pairs={{1,0},{2,1},{3,2},{4,3},{5,4},{6,5},{7,6},{8,7},{9,8},{10,9},{11,1... | collective-permute-start | bytes 1572872 | tf_op jit(solution)/shard_map/halo_fields/ppermute | solution.py:362
  11.2 1.0 copy-start.6
  13.1 36.6 %all-to-all-start = ((f32[256,2,2,128]{3,2,1,0:T(2,128)}), f32[256,2,2,128]{3,2,1,0:T(2,128)S(1)}, u32[]{:S(2)}, u32[]{:S(2)}) async-start(f32[256,2,2,128]{3,2,1,0:T(2,128)} %bitcast.14), calls=%async_computation | async-start | bytes 1048576 | tf_op jit(solution)/shard_map/spread_velocity/all_to_all | solution.py:384
  23.8 36.7 %copy-start = (f32[1,8,64,128]{3,2,1,0:T(8,128)S(1)}, f32[1,8,64,128]{3,2,1,0:T(8,128)}, u32[]{:S(2)}) copy-start(f32[1,8,64,128]{3,2,1,0:T(8,128)} %param.20) | copy-start | bytes 786436
  23.8 36.7 %copy-start.1 = (f32[1,8,64,128]{3,2,1,0:T(8,128)S(1)}, f32[1,8,64,128]{3,2,1,0:T(8,128)}, u32[]{:S(2)}) copy-start(f32[1,8,64,128]{3,2,1,0:T(8,128)} %param.21) | copy-start | bytes 786436
  51.5 18.9 %copy-start.10 = (s32[1,256]{1,0:T(1,128)S(1)}, s32[1,256]{1,0:T(1,128)}, u32[]{:S(2)}) copy-start(s32[1,256]{1,0:T(1,128)} %param.16) | copy-start | bytes 3076
  51.5 35.3 %copy-start.3 = (f32[1,8,64,128]{3,2,1,0:T(8,128)S(1)}, f32[1,8,64,128]{3,2,1,0:T(8,128)}, u32[]{:S(2)}) copy-start(f32[1,8,64,128]{3,2,1,0:T(8,128)} %param.18) | copy-start | bytes 786436
  51.5 35.3 %copy-start.5 = (f32[1,8,64,128]{3,2,1,0:T(8,128)S(1)}, f32[1,8,64,128]{3,2,1,0:T(8,128)}, u32[]{:S(2)}) copy-start(f32[1,8,64,128]{3,2,1,0:T(8,128)} %param.19) | copy-start | bytes 786436
  51.5 35.3 %copy-start.7 = (f32[1,8,256]{2,1,0:T(8,128)S(1)}, f32[1,8,256]{2,1,0:T(8,128)}, u32[]{:S(2)}) copy-start(f32[1,8,256]{2,1,0:T(8,128)} %param.17) | copy-start | bytes 24580
  51.5 35.3 %copy-start.8 = (f32[1,8]{1,0:T(1,128)S(1)}, f32[1,8]{1,0:T(1,128)}, u32[]{:S(2)}) copy-start(f32[1,8]{1,0:T(1,128)} %param.15) | copy-start | bytes 100
  51.5 35.2 %all-to-all-start.1 = ((f32[256,3,2,128]{3,2,1,0:T(2,128)}), f32[256,3,2,128]{3,2,1,0:T(2,128)S(1)}, u32[]{:S(2)}, u32[]{:S(2)}) async-start(f32[256,3,2,128]{3,2,1,0:T(2,128)} %bitcast.18), calls=%async_computation.1 | async-start | bytes 1572864 | tf_op jit(solution)/shard_map/deliver_velocity/all_to_all | solution.py:389
  61.4 36.3 %collective-permute-start.4 = (f32[15,64,128]{2,1,0:T(8,128)}, f32[15,64,128]{2,1,0:T(8,128)S(1)}, u32[]{:S(2)}, u32[]{:S(2)}) collective-permute-start(f32[15,64,128]{2,1,0:T(8,128)} %halo_fields.4), channel_id=1, source_target_pairs={{0,1},{1,2},{2,3},{3,4},{4,5},{5,6},{6,7},{7,8},{8,9},{9,10},{10,1... | collective-permute-start | bytes 1474568 | tf_op jit(solution)/shard_map/halo_fields/ppermute | solution.py:362
  64.9 35.6 %collective-permute-start.5 = (f32[15,64,128]{2,1,0:T(8,128)}, f32[15,64,128]{2,1,0:T(8,128)}, u32[]{:S(2)}, u32[]{:S(2)}) collective-permute-start(f32[15,64,128]{2,1,0:T(8,128)} %halo_fields.5), channel_id=1, source_target_pairs={{1,0},{2,1},{3,2},{4,3},{5,4},{6,5},{7,6},{8,7},{9,8},{10,9},{11,1... | collective-permute-start | bytes 1474568 | tf_op jit(solution)/shard_map/halo_fields/ppermute | solution.py:362
  91.7 8.8 %collective-permute-start.2 = (f32[8,256]{1,0:T(8,128)S(1)}, f32[8,256]{1,0:T(8,128)S(1)}, u32[]{:S(2)}, u32[]{:S(2)}) collective-permute-start(f32[8,256]{1,0:T(8,128)S(1)} %get-tuple-element.13.ro), channel_id=1, source_target_pairs={{0,1},{1,2},{2,3},{3,4},{4,5},{5,6},{6,7},{7,8},{8,9},{9,10},{10,1... | collective-permute-start | bytes 24584 | tf_op jit(solution)/shard_map/residuals/ppermute | solution.py:362
  93.5 7.2 %collective-permute-start.3 = (f32[8,256]{1,0:T(8,128)S(1)}, f32[8,256]{1,0:T(8,128)S(1)}, u32[]{:S(2)}, u32[]{:S(2)}) collective-permute-start(f32[8,256]{1,0:T(8,128)S(1)} %get-tuple-element.13.ro), channel_id=1, source_target_pairs={{1,0},{2,1},{3,2},{4,3},{5,4},{6,5},{7,6},{8,7},{9,8},{10,9},{11,1... | collective-permute-start | bytes 24584 | tf_op jit(solution)/shard_map/residuals/ppermute | solution.py:362
